TPU v7x, 32 devices: a whole 2x2x4 slice. The times are simulated.
32 devices in a mesh: tm: 8 (over y, x, core), panel: 4 (over z).
Axes of the slice: x: 2, y: 2, z: 4, core: 2. Of those that a mesh axis runs over, the one named last changes fastest.
Arguments:
- transitions: float32 [32, 512, 512], P('tm', 'panel'), may hold values from -1 to 1.1, as said below
- offsets: float32 [32, 512], P('tm', 'panel'), may hold values from -1.2 to 1.2
- noise_cov: float32 [32, 512, 512], P('tm', 'panel'), may hold values from -0.05 to 0.2, as said below
Outputs:
- smoothed_means: float32 [32, 512], P('tm', 'panel')
- smoothed_covs: float32 [32, 512, 512], P('tm', 'panel')
Inputs may be any that keep to these rules, and one draw needn't show every extreme that they name: `transitions`: each row is a rate times a row of a near-identity matrix. `noise_cov`: symmetric.
All inputs are finite; a program needn't handle non-finite values.
Results may differ from a plain program's by a relative error of at most 0.00027.
Values sent between devices are 32-bit elements; how exact they have to be, the bound alone decides.
A program may use at most 128 MiB of HBM per device.

v0:
```python
import jax
import jax.numpy as jnp
from jax import lax
from jax.sharding import PartitionSpec as P


def prefix(array, axis, combine, identity):
    peers, index = (lax.axis_size(axis), lax.axis_index(axis))
    everything = jax.tree.map(lambda part: lax.all_gather(part, axis), array)
    start = jax.tree.map(
        lambda part, zero: jnp.broadcast_to(jnp.asarray(zero, part.dtype), part.shape),
        array,
        identity,
    )

    def step(k, before):
        at = peers - 1 - k
        reached = at > index
        new = combine(before, jax.tree.map(lambda part: part[at], everything))
        return jax.tree.map(lambda a, b: jnp.where(reached, a, b), new, before)

    return lax.fori_loop(0, peers, step, start)


def product(left, right):
    return jnp.dot(left, right, precision=lax.Precision.HIGHEST, preferred_element_type=jnp.float32)


def pick(stack, index):
    return lax.dynamic_index_in_dim(stack, index, 0, keepdims=False)


def place(stack, value, index):
    return lax.dynamic_update_index_in_dim(stack, value, index, 0)


def per_device(transitions, offsets, noise_cov):
    steps = transitions.shape[0]
    entire_transition_matrix = lax.all_gather(transitions, "panel", axis=1, tiled=True)

    def reduce_step(count, state):
        acc_gain, acc_offset, acc_cov = (state[0], state[1], state[2])
        index = steps - 2 - count
        whole_gain, whole_offset, complete_covariance = (
            lax.all_gather(acc_gain, "panel", axis=0, tiled=True),
            lax.all_gather(acc_offset, "panel", axis=0, tiled=True),
            lax.all_gather(acc_cov, "panel", axis=0, tiled=True),
        )
        rows_gain = pick(transitions, index)
        new_gain = product(rows_gain, whole_gain)
        new_offset = product(rows_gain, whole_offset) + pick(offsets, index)
        new_cov = product(
            product(rows_gain, complete_covariance), pick(entire_transition_matrix, index).T
        ) + pick(noise_cov, index)
        return (new_gain, new_offset, new_cov)

    start = (transitions[steps - 1], offsets[steps - 1], noise_cov[steps - 1])
    reduced = lax.fori_loop(0, steps - 1, reduce_step, start)
    total = (reduced[0], reduced[1], reduced[2])
    whole = (
        lax.all_gather(total[0], "panel", axis=0, tiled=True),
        lax.all_gather(total[1], "panel", axis=0, tiled=True),
        lax.all_gather(total[2], "panel", axis=0, tiled=True),
    )
    width = whole[0].shape[0]
    identity = (
        jnp.eye(width, dtype=jnp.float32),
        jnp.zeros((width,), jnp.float32),
        jnp.zeros((width, width), jnp.float32),
    )

    def join(earlier, later):
        gain_a, offset_a, cov_a = earlier
        gain_b, offset_b, cov_b = later
        return (
            product(gain_b, gain_a),
            product(gain_b, offset_a) + offset_b,
            product(product(gain_b, cov_a), gain_b.T) + cov_b,
        )

    carry = prefix((whole[0], whole[1], whole[2]), "tm", join, identity)
    next_mean, successor_spread_matrix = (carry[1], carry[2])

    def smooth(index, whole_mean, complete_covariance):
        rows_gain = pick(transitions, index)
        mean_rows = product(rows_gain, whole_mean) + pick(offsets, index)
        cov_rows = product(
            product(rows_gain, complete_covariance), pick(entire_transition_matrix, index).T
        ) + pick(noise_cov, index)
        return (mean_rows, cov_rows)

    last_mean, last_cov = smooth(steps - 1, next_mean, successor_spread_matrix)
    means = jnp.zeros(offsets.shape, jnp.float32)
    covs = jnp.zeros(noise_cov.shape, jnp.float32)
    means = place(means, last_mean, steps - 1)
    covs = place(covs, last_cov, steps - 1)

    def back_step(count, state):
        means_now, present_covariances, mean_rows, cov_rows = state
        index = steps - 2 - count
        whole_mean, complete_covariance = (
            lax.all_gather(mean_rows, "panel", axis=0, tiled=True),
            lax.all_gather(cov_rows, "panel", axis=0, tiled=True),
        )
        new_mean, new_cov = smooth(index, whole_mean, complete_covariance)
        means_now = place(means_now, new_mean, index)
        present_covariances = place(present_covariances, new_cov, index)
        return (means_now, present_covariances, new_mean, new_cov)

    result = lax.fori_loop(0, steps - 1, back_step, (means, covs, last_mean, last_cov))
    return (result[0], result[1])


def solution(mesh):
    placed = (P("tm", "panel", None), P("tm", "panel"), P("tm", "panel", None))
    return jax.shard_map(
        per_device,
        mesh=mesh,
        in_specs=placed,
        out_specs=(P("tm", "panel"), P("tm", "panel", None)),
        check_vma=False,
    )
```

profile of v0, /device:TPU:0, one launch (start us, length us, event | category | flops | bytes accessed | tf_op | source)
XLA Modules:
  0.0 638.1 jit_solution(11995642334286684350)
XLA Ops:
  9.7 83.4 %all-gather.20.cloned.1.call-done = f32[4,512,512]{2,1,0:T(8,128)} async-done(((f32[4,128,512]{2,1,0:T(8,128)}), f32[4,512,512]{2,1,0:T(8,128)}) %all-gather.20.cloned.1.call-update) | async-done | bytes 4194320 | tf_op jit(solution)/shard_map/all_gather | solution.py:39
  93.1 182.8 %while.58 = (s32[]{:T(128)}, f32[128,512]{1,0:T(8,128)S(1)}, f32[128]{0:T(128)S(1)}, f32[128,512]{1,0:T(8,128)S(1)}, f32[4,128,512]{2,1,0:T(8,128)}, /*index=5*/...) while((s32[]{:T(128)}, f32[128,512]{1,0:T(8,128)S(1)}, ...), condition=%wide.region_1.2_spmd, body=%wide.region_0.1_spmd.sunk | while | flops 1208811648 | bytes 15212339 | solution.py:58
  94.5 8.1 %all-gather.9 = f32[4,1,128]{2,1,0:T(1,128)S(1)} all-gather(f32[1,1,128]{2,1,0:T(1,128)S(1)} %bitcast.181), channel_id=1, replica_groups=mesh['tm'=8,'panel'=4] {'panel'}, dimensions={0}, use_global_device_ids=true | all-gather | bytes 2560 | tf_op jit(solution)/shard_map/while/body/eval_jaxpr/all_gather | solution.py:46
  103.8 18.1 %all-gather.32.cloned.1.call-done = f32[512,512]{1,0:T(8,128)} async-done(((f32[128,512]{1,0:T(8,128)}), f32[512,512]{1,0:T(8,128)}) %all-gather.32.cloned.1.call-update) | async-done | bytes 1048592 | tf_op jit(solution)/shard_map/while/body/eval_jaxpr/all_gather | solution.py:47
  122.0 2.0 fusion.95
  124.0 2.4 convolution_add_fusion.5
  126.4 25.1 %all-gather.30.cloned.1.call-done = f32[512,512]{1,0:T(8,128)} async-done(((f32[128,512]{1,0:T(8,128)}), f32[512,512]{1,0:T(8,128)}) %all-gather.30.cloned.1.call-update) | async-done | bytes 1048592 | tf_op jit(solution)/shard_map/while/body/eval_jaxpr/all_gather | solution.py:45
  151.6 2.0 fusion.93
  154.9 9.4 %all-gather.9 = f32[4,1,128]{2,1,0:T(1,128)S(1)} all-gather(f32[1,1,128]{2,1,0:T(1,128)S(1)} %bitcast.181), channel_id=1, replica_groups=mesh['tm'=8,'panel'=4] {'panel'}, dimensions={0}, use_global_device_ids=true | all-gather | bytes 2560 | tf_op jit(solution)/shard_map/while/body/eval_jaxpr/all_gather | solution.py:46
  165.6 17.6 %all-gather.32.cloned.1.call-done = f32[512,512]{1,0:T(8,128)} async-done(((f32[128,512]{1,0:T(8,128)}), f32[512,512]{1,0:T(8,128)}) %all-gather.32.cloned.1.call-update) | async-done | bytes 1048592 | tf_op jit(solution)/shard_map/while/body/eval_jaxpr/all_gather | solution.py:47
  183.2 2.0 fusion.95
  185.2 2.4 convolution_add_fusion.5
  187.7 25.0 %all-gather.30.cloned.1.call-done = f32[512,512]{1,0:T(8,128)} async-done(((f32[128,512]{1,0:T(8,128)}), f32[512,512]{1,0:T(8,128)}) %all-gather.30.cloned.1.call-update) | async-done | bytes 1048592 | tf_op jit(solution)/shard_map/while/body/eval_jaxpr/all_gather | solution.py:45
  212.6 2.0 fusion.93
  216.2 9.4 %all-gather.9 = f32[4,1,128]{2,1,0:T(1,128)S(1)} all-gather(f32[1,1,128]{2,1,0:T(1,128)S(1)} %bitcast.181), channel_id=1, replica_groups=mesh['tm'=8,'panel'=4] {'panel'}, dimensions={0}, use_global_device_ids=true | all-gather | bytes 2560 | tf_op jit(solution)/shard_map/while/body/eval_jaxpr/all_gather | solution.py:46
  226.8 17.5 %all-gather.32.cloned.1.call-done = f32[512,512]{1,0:T(8,128)} async-done(((f32[128,512]{1,0:T(8,128)}), f32[512,512]{1,0:T(8,128)}) %all-gather.32.cloned.1.call-update) | async-done | bytes 1048592 | tf_op jit(solution)/shard_map/while/body/eval_jaxpr/all_gather | solution.py:47
  244.3 2.0 fusion.95
  246.3 2.4 convolution_add_fusion.5
  248.7 25.1 %all-gather.30.cloned.1.call-done = f32[512,512]{1,0:T(8,128)} async-done(((f32[128,512]{1,0:T(8,128)}), f32[512,512]{1,0:T(8,128)}) %all-gather.30.cloned.1.call-update) | async-done | bytes 1048592 | tf_op jit(solution)/shard_map/while/body/eval_jaxpr/all_gather | solution.py:45
  273.9 2.0 fusion.93
  277.5 28.9 %all-gather.22.cloned.1.call-done = f32[512,512]{1,0:T(8,128)} async-done(((f32[128,512]{1,0:T(8,128)}), f32[512,512]{1,0:T(8,128)}) %all-gather.22.cloned.1.call-update) | async-done | bytes 1048592 | tf_op jit(solution)/shard_map/all_gather | solution.py:61
  306.4 29.0 %all-gather.24.cloned.1.call-done = f32[512,512]{1,0:T(8,128)} async-done(((f32[128,512]{1,0:T(8,128)}), f32[512,512]{1,0:T(8,128)}) %all-gather.24.cloned.1.call-update) | async-done | bytes 1048592 | tf_op jit(solution)/shard_map/all_gather | solution.py:63
  335.5 9.4 %all-gather.5 = f32[4,1,128]{2,1,0:T(1,128)S(1)} all-gather(f32[1,1,128]{2,1,0:T(1,128)S(1)} %bitcast.182), channel_id=1, replica_groups=mesh['tm'=8,'panel'=4] {'panel'}, dimensions={0}, use_global_device_ids=true | all-gather | bytes 2560 | tf_op jit(solution)/shard_map/all_gather | solution.py:62
  344.9 9.0 %all-gather.6 = f32[8,1,512]{2,1,0:T(1,128)S(1)} all-gather(f32[1,1,512]{2,1,0:T(1,128)S(1)} %bitcast.183), channel_id=3, replica_groups=mesh['tm'=8,'panel'=4] {'tm'}, dimensions={0}, use_global_device_ids=true | all-gather | bytes 18432 | tf_op jit(solution)/shard_map/all_gather | solution.py:9
  353.9 37.2 %all-gather.26.cloned.1.call-done = f32[4096,512]{1,0:T(8,128)} async-done(((f32[512,512]{1,0:T(8,128)}), f32[4096,512]{1,0:T(8,128)}) %all-gather.26.cloned.1.call-update) | async-done | bytes 8388624 | tf_op jit(solution)/shard_map/all_gather | solution.py:9
  391.1 56.3 %all-gather.28.cloned.1.call-done = f32[4096,512]{1,0:T(8,128)} async-done(((f32[512,512]{1,0:T(8,128)}), f32[4096,512]{1,0:T(8,128)}) %all-gather.28.cloned.1.call-update) | async-done | bytes 8388624 | tf_op jit(solution)/shard_map/all_gather | solution.py:9
  447.4 73.8 %while.60 = (s32[]{:T(128)}, f32[512]{0:T(512)S(1)}, f32[512,512]{1,0:T(8,128)S(1)}, s32[]{:T(128)}, f32[8,512,512]{2,1,0:T(8,128)}, /*index=5*/f32[8,512]{1,0:T...) while((s32[]{:T(128)}, f32[512]{0:T(512)S(1)}, ...), condition=%wide.region_3.4_spmd.clone, body=%wide.region_2.3_spmd.clone.sunk | while | flops 3225421824 | bytes 9459901 | solution.py:22
  447.4 3.2 fusion.110
  450.6 3.8 fusion.111
  454.4 2.2 fusion.109
  456.7 3.1 fusion.110
  459.8 3.8 fusion.111
  463.7 2.2 fusion.109
  465.9 3.1 fusion.110
  469.0 3.8 fusion.111
  472.9 2.2 fusion.109
  475.2 3.1 fusion.110
  478.3 3.8 fusion.111
  482.1 2.2 fusion.109
  484.4 3.1 fusion.110
  487.5 3.8 fusion.111
  491.3 2.2 fusion.109
  493.6 3.1 fusion.110
  496.7 3.8 fusion.111
  500.6 2.2 fusion.109
  502.8 3.1 fusion.110
  505.9 3.8 fusion.111
  509.8 2.2 fusion.109
  512.0 3.1 fusion.110
  515.1 3.8 fusion.111
  519.0 2.2 fusion.109
  523.3 2.6 convolution_add_fusion.3
  526.1 104.4 %while.59 = (s32[]{:T(128)}, f32[4,128]{1,0:T(4,128)S(1)}, f32[4,128,512]{2,1,0:T(8,128)S(1)}, f32[128]{0:T(128)S(1)}, f32[128,512]{1,0:T(8,128)S(1)}, /*index=5...) while((s32[]{:T(128)}, f32[4,128]{1,0:T(4,128)S(1)}, ...), condition=%wide.region_5.6_spmd, body=%wide.region_4.5_spmd.sunk | while | flops 806158464 | bytes 8921847 | solution.py:110
  526.8 10.8 %all-gather.10 = f32[4,1,128]{2,1,0:T(1,128)S(1)} all-gather(f32[1,1,128]{2,1,0:T(1,128)S(1)} %bitcast.178), channel_id=1, replica_groups=mesh['tm'=8,'panel'=4] {'panel'}, dimensions={0}, use_global_device_ids=true | all-gather | bytes 2560 | tf_op jit(solution)/shard_map/while/body/eval_jaxpr/all_gather | solution.py:102
  538.0 18.7 %all-gather.34.cloned.1.call-done = f32[512,512]{1,0:T(8,128)} async-done(((f32[128,512]{1,0:T(8,128)}), f32[512,512]{1,0:T(8,128)}) %all-gather.34.cloned.1.call-update) | async-done | bytes 1048592 | tf_op jit(solution)/shard_map/while/body/eval_jaxpr/all_gather | solution.py:103
  556.8 1.9 fusion.102
  558.7 2.4 bitcast_dynamic-update-slice_fusion.2
  561.9 9.4 %all-gather.10 = f32[4,1,128]{2,1,0:T(1,128)S(1)} all-gather(f32[1,1,128]{2,1,0:T(1,128)S(1)} %bitcast.178), channel_id=1, replica_groups=mesh['tm'=8,'panel'=4] {'panel'}, dimensions={0}, use_global_device_ids=true | all-gather | bytes 2560 | tf_op jit(solution)/shard_map/while/body/eval_jaxpr/all_gather | solution.py:102
  571.7 19.9 %all-gather.34.cloned.1.call-done = f32[512,512]{1,0:T(8,128)} async-done(((f32[128,512]{1,0:T(8,128)}), f32[512,512]{1,0:T(8,128)}) %all-gather.34.cloned.1.call-update) | async-done | bytes 1048592 | tf_op jit(solution)/shard_map/while/body/eval_jaxpr/all_gather | solution.py:103
  591.6 1.9 fusion.102
  593.6 2.4 bitcast_dynamic-update-slice_fusion.2
  596.8 9.4 %all-gather.10 = f32[4,1,128]{2,1,0:T(1,128)S(1)} all-gather(f32[1,1,128]{2,1,0:T(1,128)S(1)} %bitcast.178), channel_id=1, replica_groups=mesh['tm'=8,'panel'=4] {'panel'}, dimensions={0}, use_global_device_ids=true | all-gather | bytes 2560 | tf_op jit(solution)/shard_map/while/body/eval_jaxpr/all_gather | solution.py:102
  606.5 19.6 %all-gather.34.cloned.1.call-done = f32[512,512]{1,0:T(8,128)} async-done(((f32[128,512]{1,0:T(8,128)}), f32[512,512]{1,0:T(8,128)}) %all-gather.34.cloned.1.call-update) | async-done | bytes 1048592 | tf_op jit(solution)/shard_map/while/body/eval_jaxpr/all_gather | solution.py:103
  628.1 2.4 bitcast_dynamic-update-slice_fusion.2
  (101 shorter events, 20.4 us)
Async XLA Ops:
  7.2 85.9 %all-gather.20.cloned.1.call-start = ((), (), s32[]{:S(2)}) async-start(), calls=%async_computation | async-start | bytes 5242880 | tf_op jit(solution)/shard_map/all_gather | solution.py:39
  93.1 0.7 copy-start.2
  93.1 0.8 copy-start.4
  93.1 28.9 %all-gather.32.cloned.1.call-start = ((), (), s32[]{:S(2)}) async-start(), calls=%async_computation.6 | async-start | bytes 1310720 | tf_op jit(solution)/shard_map/while/body/eval_jaxpr/all_gather | solution.py:47
  93.8 57.8 %all-gather.30.cloned.1.call-start = ((), (), s32[]{:S(2)}) async-start(), calls=%async_computation.5 | async-start | bytes 1310720 | tf_op jit(solution)/shard_map/while/body/eval_jaxpr/all_gather | solution.py:45
  153.6 0.7 copy-start.2
  153.6 0.8 copy-start.4
  153.6 29.6 %all-gather.32.cloned.1.call-start = ((), (), s32[]{:S(2)}) async-start(), calls=%async_computation.6 | async-start | bytes 1310720 | tf_op jit(solution)/shard_map/while/body/eval_jaxpr/all_gather | solution.py:47
  154.3 58.3 %all-gather.30.cloned.1.call-start = ((), (), s32[]{:S(2)}) async-start(), calls=%async_computation.5 | async-start | bytes 1310720 | tf_op jit(solution)/shard_map/while/body/eval_jaxpr/all_gather | solution.py:45
  214.7 0.7 copy-start.2
  214.7 0.8 copy-start.4
  214.7 29.6 %all-gather.32.cloned.1.call-start = ((), (), s32[]{:S(2)}) async-start(), calls=%async_computation.6 | async-start | bytes 1310720 | tf_op jit(solution)/shard_map/while/body/eval_jaxpr/all_gather | solution.py:47
  215.4 58.4 %all-gather.30.cloned.1.call-start = ((), (), s32[]{:S(2)}) async-start(), calls=%async_computation.5 | async-start | bytes 1310720 | tf_op jit(solution)/shard_map/while/body/eval_jaxpr/all_gather | solution.py:45
  275.9 0.7 copy-start.5
  275.9 0.8 copy-start.3
  275.9 30.4 %all-gather.22.cloned.1.call-start = ((), (), s32[]{:S(2)}) async-start(), calls=%async_computation.1 | async-start | bytes 1310720 | tf_op jit(solution)/shard_map/all_gather | solution.py:61
  276.7 58.7 %all-gather.24.cloned.1.call-start = ((), (), s32[]{:S(2)}) async-start(), calls=%async_computation.2 | async-start | bytes 1310720 | tf_op jit(solution)/shard_map/all_gather | solution.py:63
  277.4 113.7 %all-gather.26.cloned.1.call-start = ((), (), s32[]{:S(2)}) async-start(), calls=%async_computation.3 | async-start | bytes 9437184 | tf_op jit(solution)/shard_map/all_gather | solution.py:9
  306.4 141.0 %all-gather.28.cloned.1.call-start = ((), (), s32[]{:S(2)}) async-start(), calls=%async_computation.4 | async-start | bytes 9437184 | tf_op jit(solution)/shard_map/all_gather | solution.py:9
  447.4 73.8 %copy-start = (f32[4,128,512]{2,1,0:T(8,128)S(1)}, f32[4,128,512]{2,1,0:T(8,128)}, u32[]{:S(2)}) copy-start(f32[4,128,512]{2,1,0:T(8,128)} %get-tuple-element.952) | copy-start | bytes 3145732
  447.4 75.7 %copy-start.7 = (f32[4,128]{1,0:T(4,128)S(1)}, f32[4,128]{1,0:T(4,128)}, u32[]{:S(2)}) copy-start(f32[4,128]{1,0:T(4,128)} %get-tuple-element.977) | copy-start | bytes 6148
  526.1 0.7 copy-start.1
  526.1 30.6 %all-gather.34.cloned.1.call-start = ((), (), s32[]{:S(2)}) async-start(), calls=%async_computation.7 | async-start | bytes 1310720 | tf_op jit(solution)/shard_map/while/body/eval_jaxpr/all_gather | solution.py:103
  561.1 0.7 copy-start.1
  561.2 30.5 %all-gather.34.cloned.1.call-start = ((), (), s32[]{:S(2)}) async-start(), calls=%async_computation.7 | async-start | bytes 1310720 | tf_op jit(solution)/shard_map/while/body/eval_jaxpr/all_gather | solution.py:103
  596.0 0.7 copy-start.1
  596.0 30.1 %all-gather.34.cloned.1.call-start = ((), (), s32[]{:S(2)}) async-start(), calls=%async_computation.7 | async-start | bytes 1310720 | tf_op jit(solution)/shard_map/while/body/eval_jaxpr/all_gather | solution.py:103
  630.5 1.0 copy-start.6
  630.6 1.0 copy-start.8
Sparse Core Ops, SparseCore 0:
  9.6 83.4 all-gather.19
  95.5 26.4 all-gather.31
  124.1 27.4 all-gather.29
  155.7 27.4 all-gather.31
  185.2 27.4 all-gather.29
  216.8 27.4 all-gather.31
  246.4 27.4 all-gather.29
  278.9 27.4 all-gather.21
  307.9 27.4 all-gather.23
  337.1 53.9 all-gather.25
  393.0 54.3 all-gather.27
  528.8 27.9 all-gather.33
  564.2 27.4 all-gather.33
  598.7 27.4 all-gather.33
where the time goes:
time: 640 us; the launch traced here: 638 us
  waiting for transfers between devices  425 us (66%)
  matrix products  115 us (18%)
  blocking collectives  75 us (12%)
  between operations  13.9 us (2%)
  local copies, waits for them, and re-layouts  7.88 us (1%)
    dot_general x48, matrix products, product(): jnp.dot(left, right, precision=lax.Precision.HIGHEST, preferred_element_t...  115 us
    all_gather x2, waiting for transfers between devices, prefix(): everything = jax.tree.map(lambda part: lax.all_gather(part, axis), array)  93.5 us
    all_gather x1, waiting for transfers between devices, per_device(): lax.all_gather(transitions, 'panel', axis=1, tiled=True)  83.4 us
    all_gather x3, waiting for transfers between devices, reduce_step(): lax.all_gather(acc_gain, 'panel', axis=0, tiled=True)  75.2 us
    all_gather x3, waiting for transfers between devices, back_step(): lax.all_gather(cov_rows, 'panel', axis=0, tiled=True)  58.3 us
    all_gather x3, waiting for transfers between devices, reduce_step(): lax.all_gather(acc_cov, 'panel', axis=0, tiled=True)  53.2 us
    all_gather x3, blocking collectives, back_step(): lax.all_gather(mean_rows, 'panel', axis=0, tiled=True)  29.6 us
    all_gather x1, waiting for transfers between devices, per_device(): lax.all_gather(total[2], 'panel', axis=0, tiled=True)  29 us
  transfers between devices with their start and end apart: 14, of which 14 were waited for; matrix products, arithmetic and copies ran while one was open for 3% of the time, Pallas kernels for 0%

commit v1 on v0

v1 whole, which is shorter than its diff:
```python
import jax
import jax.numpy as jnp
from jax import lax
from jax.sharding import PartitionSpec as P


def product(left, right):
    return jnp.dot(left, right, precision=lax.Precision.HIGH, preferred_element_type=jnp.float32)


def product_t(left, right):
    return lax.dot_general(
        left, right, (((1,), (1,)), ((), ())),
        precision=lax.Precision.HIGH, preferred_element_type=jnp.float32,
    )


def matvec(matrix, vector):
    return jnp.sum(matrix * vector[None, :], axis=1)


def send(value, pairs):
    return lax.ppermute(value, "tm", pairs)


def spread(value, core, distance, blocks, groups):
    half = value.shape[0] // 2
    own = jnp.where(core == 0, value[:half], value[half:])
    got = None
    for pair in range(distance // 2):
        pairs = [
            (base + distance + c, base + 2 * pair + c) for base in groups for c in range(2)
        ]
        part = send(own, pairs)
        got = part if got is None else got + part
    other = send(got, [(t, t ^ 1) for t in range(blocks)])
    return jnp.where(
        core == 0, jnp.concatenate([got, other]), jnp.concatenate([other, got])
    )


def later_state(gains, offsets, covs):
    blocks = lax.axis_size("tm")
    me = lax.axis_index("tm")
    core = me % 2
    swap = [(t, t ^ 1) for t in range(blocks)]
    r_gain, r_offset, r_cov = send(gains, swap), send(offsets, swap), send(covs, swap)
    lower = core == 0
    eye = jnp.eye(gains.shape[0], dtype=jnp.float32)
    x_gain = jnp.where(lower, r_gain, eye)
    x_offset = jnp.where(lower, r_offset, 0.0)
    x_cov = jnp.where(lower, r_cov, 0.0)
    first = jnp.where(lower, gains, r_gain)
    g_offset = matvec(first, jnp.where(lower, r_offset, offsets)) + jnp.where(
        lower, offsets, r_offset
    )
    g_cov = product_t(product(first, jnp.where(lower, r_cov, covs)), first) + jnp.where(
        lower, covs, r_cov
    )
    g_gain = product(first, jnp.where(lower, r_gain, gains))
    distance = 2
    while distance < blocks:
        last = 2 * distance == blocks
        groups = list(range(0, blocks, 2 * distance))
        r_cov = spread(g_cov, core, distance, blocks, groups)
        r_offset = spread(g_offset, core, distance, blocks, groups)
        lower = (me // distance) % 2 == 0
        new_cov = product_t(product(x_gain, r_cov), x_gain) + x_cov
        new_offset = matvec(x_gain, r_offset) + x_offset
        if not last:
            r_gain = spread(g_gain, core, distance, blocks, groups[:-1])
            g_offset = matvec(g_gain, r_offset) + g_offset
            g_cov = product_t(product(g_gain, r_cov), g_gain) + g_cov
            g_gain = product(g_gain, r_gain)
            x_gain = jnp.where(lower, product(x_gain, r_gain), x_gain)
        x_cov = jnp.where(lower, new_cov, x_cov)
        x_offset = jnp.where(lower, new_offset, x_offset)
        distance *= 2
    return x_offset, x_cov


def per_device(transitions, offsets, noise_cov):
    steps, rows = transitions.shape[:2]
    start = lax.axis_index("panel") * rows
    whole = {}
    for k in [*range(steps - 2, -1, -1), steps - 1]:
        whole[k] = lax.all_gather(transitions[k], "panel", axis=0, tiled=True)
    all_offsets = lax.all_gather(offsets, "panel", axis=1, tiled=True)
    cov = noise_cov[steps - 1]
    offset = all_offsets[steps - 1]
    gain = whole[steps - 1]
    covs, gains, means = [cov], [gain], [offset]
    for k in range(steps - 2, -1, -1):
        columns = product_t(whole[k], cov)
        mine = lax.all_to_all(columns, "panel", split_axis=0, concat_axis=1, tiled=True)
        cov = product_t(mine, whole[k]) + noise_cov[k]
        gain = product(whole[k], gain)
        offset = matvec(whole[k], offset) + all_offsets[k]
        covs.append(cov)
        gains.append(gain)
        means.append(offset)
    whole_cov = lax.all_gather(cov, "panel", axis=0, tiled=True)
    next_mean, next_cov = later_state(gain, offset, whole_cov)
    covs, gains, means = covs[::-1], gains[::-1], means[::-1]
    own = jnp.concatenate([lax.dynamic_slice_in_dim(f, start, rows, 0) for f in gains])
    own_offsets = jnp.concatenate(
        [lax.dynamic_slice_in_dim(m, start, rows, 0) for m in means]
    )
    mean = (matvec(own, next_mean) + own_offsets).reshape(steps, rows)
    left = product(own, next_cov).reshape(steps, rows, -1)
    out = jnp.stack([product_t(left[k], gains[k]) + covs[k] for k in range(steps)])
    return mean, out


def solution(mesh):
    placed = (P("tm", "panel", None), P("tm", "panel"), P("tm", "panel", None))
    return jax.shard_map(
        per_device,
        mesh=mesh,
        in_specs=placed,
        out_specs=(P("tm", "panel"), P("tm", "panel", None)),
        check_vma=False,
    )
```

time: 640 us -> 263 us (0.41)
  waiting for transfers between devices: 425 us -> 140 us
  matrix products: 115 us -> 42.3 us
  blocking collectives: 75 us -> 21.4 us
  starting transfers between devices: 0.54 us -> 20.8 us
  local copies, waits for them, and re-layouts: 7.88 us -> 19.9 us
    all_gather x14 -> x5, waiting for transfers between devices: 422 us -> 93.2 us  [the longest x4 70 us: per_device(): whole[k] = lax.all_gather(transitions[k], 'panel', axis=0, tiled=True)]
    dot_general x48 -> x24, matrix products: 115 us -> 42.3 us  [the longest x10 25.4 us: product(): jnp.dot(left, right, precision=lax.Precision.HIGH, preferred_element_type...]
    all_gather x8 -> x1, blocking collectives: 75 us -> 21.4 us  [per_device(): all_offsets = lax.all_gather(offsets, 'panel', axis=1, tiled=True)]
    ppermute x0 -> x15, waiting for transfers between devices: none -> 32.8 us  [send(): return lax.ppermute(value, 'tm', pairs)]
    all_to_all x0 -> x3, waiting for transfers between devices: none -> 12.5 us  [per_device(): lax.all_to_all(columns, 'panel', split_axis=0, concat_axis=1, tiled=True)]
    all_to_all x0 -> x3, starting transfers between devices: none -> 10.9 us  [per_device(): lax.all_to_all(columns, 'panel', split_axis=0, concat_axis=1, tiled=True)]
    ppermute x0 -> x15, starting transfers between devices: none -> 9.77 us  [send(): return lax.ppermute(value, 'tm', pairs)]
    unnamed x13 -> x54, local copies, waits for them, and re-layouts: 1.61 us -> 9.16 us
  transfers between devices with their start and end apart: 14 -> 23, of which waited for: 14 -> 12; matrix products, arithmetic and copies ran while one was open for 3% -> 16% of each run, Pallas kernels for 0% -> 0%
where the time goes in v1:
time: 263 us; the launch traced here: 261 us
  waiting for transfers between devices  140 us (53%)
  matrix products  42.3 us (16%)
  blocking collectives  21.4 us (8%)
  starting transfers between devices  20.8 us (8%)
  local copies, waits for them, and re-layouts  19.9 us (8%)
  between operations  14.4 us (5%)
    all_gather x4, waiting for transfers between devices, per_device(): whole[k] = lax.all_gather(transitions[k], 'panel', axis=0, tiled=True)  70 us
    ppermute x15, waiting for transfers between devices, send(): return lax.ppermute(value, 'tm', pairs)  32.8 us
    dot_general x10, matrix products, product(): jnp.dot(left, right, precision=lax.Precision.HIGH, preferred_element_type...  25.4 us
    all_gather x1, waiting for transfers between devices, per_device(): whole_cov = lax.all_gather(cov, 'panel', axis=0, tiled=True)  23.1 us
    all_gather x1, blocking collectives, per_device(): all_offsets = lax.all_gather(offsets, 'panel', axis=1, tiled=True)  21.4 us
    dot_general x14, matrix products, product_t(): lax.dot_general(left, right, (((1,), (1,)), ((), ())), precision=lax.Prec...  16.9 us
    all_to_all x3, waiting for transfers between devices, per_device(): lax.all_to_all(columns, 'panel', split_axis=0, concat_axis=1, tiled=True)  12.5 us
    all_to_all x3, starting transfers between devices, per_device(): lax.all_to_all(columns, 'panel', split_axis=0, concat_axis=1, tiled=True)  10.9 us
  transfers between devices with their start and end apart: 23, of which 12 were waited for; matrix products, arithmetic and copies ran while one was open for 16% of the time, Pallas kernels for 0%

profile of v1, /device:TPU:0, one launch (start us, length us, event | category | flops | bytes accessed | tf_op | source)
XLA Modules:
  0.0 261.0 jit_solution(16757652988256290288)
XLA Ops:
  7.2 2.3 fusion.70
  9.5 0.7 all-gather.16.cloned.1.call-update
  10.3 0.7 all-gather.18.cloned.1.call-update
  11.0 29.3 %all-gather.12.cloned.1.call-done = f32[1,512,512]{2,1,0:T(8,128)} async-done(((f32[1,128,512]{2,1,0:T(8,128)}), f32[1,512,512]{2,1,0:T(8,128)}) %all-gather.12.cloned.1.call-update) | async-done | bytes 1048592 | tf_op jit(solution)/shard_map/all_gather | solution.py:87
  40.3 2.5 fusion.55
  42.8 3.4 %all-to-all-start = ((f32[4,128,128]{2,1,0:T(8,128)}), f32[4,128,128]{2,1,0:T(8,128)S(1)}, u32[]{:S(2)}, u32[]{:S(2)}) async-start(f32[4,128,128]{2,1,0:T(8,128)} %fusion.55), calls=%async_computation | async-start | bytes 524288 | tf_op jit(solution)/shard_map/all_to_all | solution.py:95
  46.8 0.8 fusion.69
  47.8 12.5 %all-to-all-done = f32[4,128,128]{2,1,0:T(8,128)S(1)} async-done(((f32[4,128,128]{2,1,0:T(8,128)}), f32[4,128,128]{2,1,0:T(8,128)S(1)}, u32[]{:S(2)}, u32[]{:S(2)}) %all-to-all-start) | async-done | bytes 262176 | tf_op jit(solution)/shard_map/all_to_all | solution.py:95
  61.0 11.5 %all-gather.16.cloned.1.call-done = f32[1,512,512]{2,1,0:T(8,128)} async-done(((f32[1,128,512]{2,1,0:T(8,128)}), f32[1,512,512]{2,1,0:T(8,128)}) %all-gather.16.cloned.1.call-update) | async-done | bytes 1048592 | tf_op jit(solution)/shard_map/all_gather | solution.py:87
  72.5 1.9 convolution_bitcast_fusion.1
  74.4 0.7 copy.64
  75.1 3.4 %all-to-all-start.1 = ((f32[4,128,128]{1,2,0:T(8,128)}), f32[4,128,128]{1,2,0:T(8,128)S(1)}, u32[]{:S(2)}, u32[]{:S(2)}) async-start(f32[4,128,128]{1,2,0:T(8,128)} %bitcast.130), calls=%async_computation.1 | async-start | bytes 524288 | tf_op jit(solution)/shard_map/all_to_all | solution.py:95
  78.6 21.4 %all_gather.22 = f32[4,512]{1,0:T(4,128)S(1)} all-gather(f32[4,128]{1,0:T(4,128)S(1)} %copy-done.23), channel_id=1, replica_groups=mesh['tm'=8,'panel'=4] {'panel'}, dimensions={1}, use_global_device_ids=true | all-gather | bytes 10240 | tf_op jit(solution)/shard_map/all_gather | solution.py:88
  100.0 1.1 copy.57
  101.1 0.8 copy.58
  101.9 0.6 convolution_add_fusion.7
  102.5 2.7 %all-gather.18.cloned.1.call-done = f32[1,512,512]{2,1,0:T(8,128)} async-done(((f32[1,128,512]{2,1,0:T(8,128)}), f32[1,512,512]{2,1,0:T(8,128)}) %all-gather.18.cloned.1.call-update) | async-done | bytes 1048592 | tf_op jit(solution)/shard_map/all_gather | solution.py:87
  105.3 1.9 convolution_bitcast_fusion
  107.2 0.7 copy.63
  107.9 4.0 %all-to-all-start.2 = ((f32[4,128,128]{1,2,0:T(8,128)}), f32[4,128,128]{1,2,0:T(8,128)}, u32[]{:S(2)}, u32[]{:S(2)}) async-start(f32[4,128,128]{1,2,0:T(8,128)} %bitcast.129), calls=%async_computation.2 | async-start | bytes 524288 | tf_op jit(solution)/shard_map/all_to_all | solution.py:95
  112.0 26.5 %all-gather.14.cloned.1.call-done = f32[1,512,512]{2,1,0:T(8,128)} async-done(((f32[1,128,512]{2,1,0:T(8,128)}), f32[1,512,512]{2,1,0:T(8,128)}) %all-gather.14.cloned.1.call-update) | async-done | bytes 1048592 | tf_op jit(solution)/shard_map/all_gather | solution.py:87
  138.5 2.2 fusion.27
  140.8 1.0 copy-done.6
  141.7 2.0 fusion.23
  143.7 2.2 convolution_add_fusion.6
  146.0 3.2 %fusion.18 = f32[512,512]{1,0:T(8,128)S(1)} fusion(f32[512,512]{0,1:T(8,128)} %fusion.23, f32[1,512,512]{2,1,0:T(8,128)S(1)} %copy-done.1), kind=kOutput, calls=%fused_computation.38 | convolution fusion | flops 805306368 | bytes 3145728 | tf_op jit(solution)/shard_map/dot_general | solution.py:8
  149.7 0.9 copy-done.2
  151.2 0.8 collective-permute-done.3
  152.3 23.1 %all-gather.10.cloned.1.call-done = f32[512,512]{0,1:T(8,128)} async-done(((f32[128,512]{0,1:T(8,128)}), f32[512,512]{0,1:T(8,128)}) %all-gather.10.cloned.1.call-update) | async-done | bytes 1048592 | tf_op jit(solution)/shard_map/all_gather | solution.py:102
  175.4 1.3 collective-permute-start.4
  176.7 4.1 %collective-permute-done.4 = f32[256]{0:T(256)S(1)} collective-permute-done((f32[256]{0:T(256)S(1)}, f32[256]{0:T(256)S(1)}, u32[]{:S(2)}, u32[]{:S(2)}) %collective-permute-start.4) | collective-permute-done | bytes 1056 | tf_op jit(solution)/shard_map/ppermute | solution.py:23
  180.9 0.8 copy.55
  182.0 1.1 multiply_reduce_fusion.1
  183.2 1.6 collective-permute-start.1
  184.8 3.1 %fusion.33 = f32[512,512]{1,0:T(8,128)S(1)} fusion(f32[512,512]{0,1:T(8,128)} %collective-permute-done.9, f32[512,512]{0,1:T(8,128)S(1)} %copy-done.11, pred[]{:T(512)S(6)} %eq.14, f32[512,512]{0,1:T(8,128)S(1)} %collective-permute-done, f32[512,512]{1,0:T(8,128)S(1)} %fusion.18), kind=kOutput, calls=%fused_computation.55 | convolution fusion | flops 805830656 | bytes 5242881 | tf_op jit(solution)/shard_map/dot_general | solution.py:8
  188.0 1.1 convolution_add_fusion.1
  189.2 1.3 collective-permute-start.10
  190.5 1.7 constant_dynamic-slice_fusion.1
  192.2 1.7 dynamic-slice_bitcast_fusion.1
  193.9 6.2 %collective-permute-done.1 = f32[256,512]{0,1:T(8,128)} collective-permute-done((f32[256,512]{0,1:T(8,128)S(1)}, f32[256,512]{0,1:T(8,128)}, u32[]{:S(2)}, u32[]{:S(2)}) %collective-permute-start.1) | collective-permute-done | bytes 524320 | tf_op jit(solution)/shard_map/ppermute | solution.py:23
  200.1 1.3 collective-permute-start.6
  201.4 0.7 collective-permute-start.7
  202.1 8.5 %collective-permute-done.10 = f32[256,512]{0,1:T(8,128)} collective-permute-done((f32[256,512]{0,1:T(8,128)S(1)}, f32[256,512]{0,1:T(8,128)}, u32[]{:S(2)}, u32[]{:S(2)}) %collective-permute-start.10) | collective-permute-done | bytes 524320 | tf_op jit(solution)/shard_map/ppermute | solution.py:23
  210.6 0.8 constant_dynamic-slice_fusion.2
  211.9 1.7 dynamic-slice_bitcast_fusion
  213.7 1.8 copy.54
  215.7 2.6 %multiply_reduce_fusion.2 = (f32[512]{0:T(512)S(1)}, f32[512,512]{0,1:T(8,128)S(1)}) fusion(f32[512]{0:T(512)S(1)} %maximum_select_fusion.8, f32[512,512]{0,1:T(8,128)S(1)} %collective-permute-done, pred[]{:T(512)S(6)} %eq.14, f32[256,512]{0,1:T(8,128)} %collective-permute-done.2, f32[256,512]{0,1:T(8,128)} %collective-permute-done.1, pred[]{:T(512)S(6)} %eq.13), kind=kOutput, calls=%fused_computation.59 | convolution fusion | flops 808451584 | bytes 3149826 | tf_op jit(solution)/shard_map/dot_general | solution.py:8
  218.4 3.5 %fusion.39 = f32[512,512]{1,0:T(8,128)S(1)} fusion(f32[512,512]{0,1:T(8,128)S(1)} %get-tuple-element.20, f32[256,512]{0,1:T(8,128)} %collective-permute-done.11, f32[256,512]{0,1:T(8,128)} %collective-permute-done.10, pred[]{:T(512)S(6)} %eq.14), kind=kOutput, calls=%fused_computation.68 | convolution fusion | flops 806092800 | bytes 3145729 | tf_op jit(solution)/shard_map/dot_general | solution.py:8
  221.9 1.1 convolution_add_fusion
  223.0 1.4 collective-permute-start.12
  224.5 0.9 collective-permute-start.13
  225.6 0.6 fusion.57
  226.2 12.7 %collective-permute-done.12 = f32[256,512]{0,1:T(8,128)S(1)} collective-permute-done((f32[256,512]{0,1:T(8,128)S(1)}, f32[256,512]{0,1:T(8,128)S(1)}, u32[]{:S(2)}, u32[]{:S(2)}) %collective-permute-start.12) | collective-permute-done | bytes 524320 | tf_op jit(solution)/shard_map/ppermute | solution.py:23
  239.1 3.4 %fusion.37 = f32[512,512]{1,0:T(8,128)S(1)} fusion(f32[512,512]{0,1:T(8,128)S(1)} %collective-permute-done, f32[256,512]{0,1:T(8,128)} %collective-permute-done.11, f32[256,512]{0,1:T(8,128)} %collective-permute-done.10, pred[]{:T(512)S(6)} %eq.14), kind=kOutput, calls=%fused_computation.66 | convolution fusion | flops 806879232 | bytes 3145729 | tf_op jit(solution)/shard_map/dot_general | solution.py:8
  242.5 1.1 fusion.38
  243.6 1.9 fusion.10
  245.5 1.0 fusion.72
  246.5 2.5 fusion.4
  249.0 0.6 fusion.1
  249.6 0.6 copy-done.5
  250.3 0.6 fusion.2
  251.2 1.0 fusion.3
  252.5 0.6 fusion
  253.2 1.3 copy.41
  (105 shorter events, 5.4 us)
Async XLA Ops:
  7.2 33.1 %copy-start.19 = (f32[4,128,512]{2,1,0:T(8,128)S(1)}, f32[4,128,512]{2,1,0:T(8,128)}, u32[]{:S(2)}) copy-start(f32[4,128,512]{2,1,0:T(8,128)} %param.5) | copy-start | bytes 3145732
  7.2 33.1 %all-gather.12.cloned.1.call-start = ((), (), s32[]{:S(2)}) async-start(), calls=%async_computation.4 | async-start | bytes 1310720 | tf_op jit(solution)/shard_map/all_gather | solution.py:87
  9.5 63.0 %all-gather.16.cloned.1.call-start = ((), (), s32[]{:S(2)}) async-start(), calls=%async_computation.6 | async-start | bytes 1310720 | tf_op jit(solution)/shard_map/all_gather | solution.py:87
  10.2 95.0 %all-gather.18.cloned.1.call-start = ((), (), s32[]{:S(2)}) async-start(), calls=%async_computation.7 | async-start | bytes 1310720 | tf_op jit(solution)/shard_map/all_gather | solution.py:87
  42.8 17.4 %all-to-all-start = ((f32[4,128,128]{2,1,0:T(8,128)}), f32[4,128,128]{2,1,0:T(8,128)S(1)}, u32[]{:S(2)}, u32[]{:S(2)}) async-start(f32[4,128,128]{2,1,0:T(8,128)} %fusion.55), calls=%async_computation | async-start | bytes 524288 | tf_op jit(solution)/shard_map/all_to_all | solution.py:95
  46.2 92.3 %all-gather.14.cloned.1.call-start = ((), (), s32[]{:S(2)}) async-start(), calls=%async_computation.5 | async-start | bytes 1310720 | tf_op jit(solution)/shard_map/all_gather | solution.py:87
  47.7 12.7 %copy-start.3 = (f32[1,512,512]{2,1,0:T(8,128)S(1)}, f32[1,512,512]{2,1,0:T(8,128)}, u32[]{:S(2)}) copy-start(f32[1,512,512]{2,1,0:T(8,128)} %all-gather.12.cloned.1.call-done) | copy-start | bytes 3145732
  72.5 6.1 %copy-start.23 = (f32[4,128]{1,0:T(4,128)S(1)}, f32[4,128]{1,0:T(4,128)}, u32[]{:S(2)}) copy-start(f32[4,128]{1,0:T(4,128)} %param.4) | copy-start | bytes 6148
  74.4 27.5 %copy-start = (f32[1,512,512]{2,1,0:T(8,128)S(1)}, f32[1,512,512]{2,1,0:T(8,128)}, u32[]{:S(2)}) copy-start(f32[1,512,512]{2,1,0:T(8,128)} %all-gather.16.cloned.1.call-done) | copy-start | bytes 3145732
  75.1 26.8 %all-to-all-start.1 = ((f32[4,128,128]{1,2,0:T(8,128)}), f32[4,128,128]{1,2,0:T(8,128)S(1)}, u32[]{:S(2)}, u32[]{:S(2)}) async-start(f32[4,128,128]{1,2,0:T(8,128)} %bitcast.130), calls=%async_computation.1 | async-start | bytes 524288 | tf_op jit(solution)/shard_map/all_to_all | solution.py:95
  102.5 4.7 %copy-start.13 = (f32[128,512]{0,1:T(8,128)}, f32[128,512]{0,1:T(8,128)S(1)}, u32[]{:S(2)}) copy-start(f32[128,512]{0,1:T(8,128)S(1)} %convolution_add_fusion.7) | copy-start | bytes 786436
  107.9 35.8 %all-to-all-start.2 = ((f32[4,128,128]{1,2,0:T(8,128)}), f32[4,128,128]{1,2,0:T(8,128)}, u32[]{:S(2)}, u32[]{:S(2)}) async-start(f32[4,128,128]{1,2,0:T(8,128)} %bitcast.129), calls=%async_computation.2 | async-start | bytes 524288 | tf_op jit(solution)/shard_map/all_to_all | solution.py:95
  112.0 63.4 %all-gather.10.cloned.1.call-start = ((), (), s32[]{:S(2)}) async-start(), calls=%async_computation.3 | async-start | bytes 1310720 | tf_op jit(solution)/shard_map/all_gather | solution.py:102
  140.8 1.0 copy-start.6
  141.7 2.0 copy-start.1
  141.7 2.0 copy-start.21
  146.0 3.3 %copy-start.4 = (f32[1,512,512]{2,1,0:T(8,128)S(1)}, f32[1,512,512]{2,1,0:T(8,128)}, u32[]{:S(2)}) copy-start(f32[1,512,512]{2,1,0:T(8,128)} %all-gather.12.cloned.1.call-done) | copy-start | bytes 3145732
  149.2 2.9 %collective-permute-start = (f32[512,512]{0,1:T(8,128)S(1)}, f32[512,512]{0,1:T(8,128)S(1)}, u32[]{:S(2)}, u32[]{:S(2)}) collective-permute-start(f32[512,512]{0,1:T(8,128)S(1)} %bitcast.131), channel_id=1, source_target_pairs={{0,4},{4,0},{8,12},{12,8},{16,20},{20,16},{24,28},{28,24},{1,5},{5... | collective-permute-start | bytes 3145736 | tf_op jit(solution)/shard_map/ppermute | solution.py:23
  149.3 1.2 copy-start.2
  150.7 1.3 collective-permute-start.3
  152.1 28.8 %copy-start.22 = (f32[1,128,512]{2,1,0:T(8,128)S(1)}, f32[1,128,512]{2,1,0:T(8,128)}, u32[]{:S(2)}) copy-start(f32[1,128,512]{2,1,0:T(8,128)} %get-tuple-element.8) | copy-start | bytes 786436
  175.4 9.4 %collective-permute-start.9 = (f32[512,512]{0,1:T(8,128)}, f32[512,512]{0,1:T(8,128)}, u32[]{:S(2)}, u32[]{:S(2)}) collective-permute-start(f32[512,512]{0,1:T(8,128)} %all-gather.10.cloned.1.call-done), channel_id=1, source_target_pairs={{0,4},{4,0},{8,12},{12,8},{16,20},{20,16},{24,28},{28,24},{1,5},{5... | collective-permute-start | bytes 3145736 | tf_op jit(solution)/shard_map/ppermute | solution.py:23
  175.4 5.5 %collective-permute-start.4 = (f32[256]{0:T(256)S(1)}, f32[256]{0:T(256)S(1)}, u32[]{:S(2)}, u32[]{:S(2)}) collective-permute-start(f32[256]{0:T(256)S(1)} %slice_select_fusion.4), channel_id=1, source_target_pairs={{8,0},{12,4},{24,16},{28,20},{9,1},{13,5},{25,17},{29,21},{10,2},{... | collective-permute-start | bytes 3080 | tf_op jit(solution)/shard_map/ppermute | solution.py:23
  180.9 1.1 collective-permute-start.5
  183.1 1.7 copy-start.11
  183.2 16.9 %collective-permute-start.1 = (f32[256,512]{0,1:T(8,128)S(1)}, f32[256,512]{0,1:T(8,128)}, u32[]{:S(2)}, u32[]{:S(2)}) collective-permute-start(f32[256,512]{0,1:T(8,128)S(1)} %slice_select_fusion.2), channel_id=1, source_target_pairs={{8,0},{12,4},{9,1},{13,5},{10,2},{14,6},{11,3},{15,7}} | collective-permute-start | bytes 1572872 | tf_op jit(solution)/shard_map/ppermute | solution.py:23
  189.1 3.1 %copy-start.8 = (f32[512,512]{0,1:T(8,128)}, f32[512,512]{0,1:T(8,128)S(1)}, u32[]{:S(2)}) copy-start(f32[512,512]{0,1:T(8,128)S(1)} %convolution_add_fusion.1) | copy-start | bytes 3145732
  189.2 21.4 %collective-permute-start.10 = (f32[256,512]{0,1:T(8,128)S(1)}, f32[256,512]{0,1:T(8,128)}, u32[]{:S(2)}, u32[]{:S(2)}) collective-permute-start(f32[256,512]{0,1:T(8,128)S(1)} %slice_select_fusion.1), channel_id=1, source_target_pairs={{8,0},{12,4},{24,16},{28,20},{9,1},{13,5},{25,17},{29,21},{10,2},{... | collective-permute-start | bytes 1572872 | tf_op jit(solution)/shard_map/ppermute | solution.py:23
  200.1 15.6 %collective-permute-start.2 = (f32[256,512]{0,1:T(8,128)}, f32[256,512]{0,1:T(8,128)}, u32[]{:S(2)}, u32[]{:S(2)}) collective-permute-start(f32[256,512]{0,1:T(8,128)} %collective-permute-done.1), channel_id=1, source_target_pairs={{0,4},{4,0},{8,12},{12,8},{16,20},{20,16},{24,28},{28,24},{1,5},{5... | collective-permute-start | bytes 1572872 | tf_op jit(solution)/shard_map/ppermute | solution.py:23
  200.1 11.3 %collective-permute-start.6 = (f32[256]{0:T(256)S(1)}, f32[256]{0:T(256)S(1)}, u32[]{:S(2)}, u32[]{:S(2)}) collective-permute-start(f32[256]{0:T(256)S(1)} %slice_select_fusion.3), channel_id=1, source_target_pairs={{16,0},{20,4},{17,1},{21,5},{18,2},{22,6},{19,3},{23,7}} | collective-permute-start | bytes 3080 | tf_op jit(solution)/shard_map/ppermute | solution.py:23
  201.4 10.0 %collective-permute-start.7 = (f32[256]{0:T(256)S(1)}, f32[256]{0:T(256)S(1)}, u32[]{:S(2)}, u32[]{:S(2)}) collective-permute-start(f32[256]{0:T(256)S(1)} %slice_select_fusion.3), channel_id=1, source_target_pairs={{16,8},{20,12},{17,9},{21,13},{18,10},{22,14},{19,11},{23,15}} | collective-permute-start | bytes 3080 | tf_op jit(solution)/shard_map/ppermute | solution.py:23
  210.6 7.8 %collective-permute-start.11 = (f32[256,512]{0,1:T(8,128)}, f32[256,512]{0,1:T(8,128)}, u32[]{:S(2)}, u32[]{:S(2)}) collective-permute-start(f32[256,512]{0,1:T(8,128)} %collective-permute-done.10), channel_id=1, source_target_pairs={{0,4},{4,0},{8,12},{12,8},{16,20},{20,16},{24,28},{28,24},{1,5},{5... | collective-permute-start | bytes 1572872 | tf_op jit(solution)/shard_map/ppermute | solution.py:23
  211.4 4.3 %collective-permute-start.8 = (f32[256]{0:T(256)S(1)}, f32[256]{0:T(256)S(1)}, u32[]{:S(2)}, u32[]{:S(2)}) collective-permute-start(f32[256]{0:T(256)S(1)} %add.104), channel_id=1, source_target_pairs={{0,4},{4,0},{8,12},{12,8},{16,20},{20,16},{24,28},{28,24},{1,5},{5... | collective-permute-start | bytes 3080 | tf_op jit(solution)/shard_map/ppermute | solution.py:23
  218.4 3.5 %copy-start.9 = (f32[512,512]{0,1:T(8,128)S(1)}, f32[512,512]{0,1:T(8,128)}, u32[]{:S(2)}) copy-start(f32[512,512]{0,1:T(8,128)} %copy-done.8) | copy-start | bytes 3145732
  222.9 2.5 copy-start.15
  222.9 2.5 copy-start.16
  222.9 2.5 copy-start.17
  223.0 2.5 copy-start.18
  223.0 15.9 %collective-permute-start.12 = (f32[256,512]{0,1:T(8,128)S(1)}, f32[256,512]{0,1:T(8,128)S(1)}, u32[]{:S(2)}, u32[]{:S(2)}) collective-permute-start(f32[256,512]{0,1:T(8,128)S(1)} %slice_select_fusion), channel_id=1, source_target_pairs={{16,0},{20,4},{17,1},{21,5},{18,2},{22,6},{19,3},{23,7}} | collective-permute-start | bytes 1572872 | tf_op jit(solution)/shard_map/ppermute | solution.py:23
  224.5 14.4 %collective-permute-start.13 = (f32[256,512]{0,1:T(8,128)S(1)}, f32[256,512]{0,1:T(8,128)S(1)}, u32[]{:S(2)}, u32[]{:S(2)}) collective-permute-start(f32[256,512]{0,1:T(8,128)S(1)} %slice_select_fusion), channel_id=1, source_target_pairs={{16,8},{20,12},{17,9},{21,13},{18,10},{22,14},{19,11},{23,15}} | collective-permute-start | bytes 1572872 | tf_op jit(solution)/shard_map/ppermute | solution.py:23
  239.0 4.6 %collective-permute-start.14 = (f32[256,512]{0,1:T(8,128)S(1)}, f32[256,512]{0,1:T(8,128)S(1)}, u32[]{:S(2)}, u32[]{:S(2)}) collective-permute-start(f32[256,512]{0,1:T(8,128)S(1)} %add.116), channel_id=1, source_target_pairs={{0,4},{4,0},{8,12},{12,8},{16,20},{20,16},{24,28},{28,24},{1,5},{5... | collective-permute-start | bytes 1572872 | tf_op jit(solution)/shard_map/ppermute | solution.py:23
  246.5 2.5 copy-start.7
  249.0 1.2 copy-start.5
  249.0 1.3 copy-start.14
  250.3 0.9 copy-start.12
  251.2 1.2 copy-start.10
  251.2 1.3 copy-start.20
Sparse Core Ops, SparseCore 0:
  9.6 30.6 all-gather.11
  41.8 30.5 all-gather.15
  74.6 30.6 all-gather.17
  106.7 31.8 all-gather.13
  146.1 29.2 all-gather.9

commit v2 on v1

--- a/solution.py
+++ b/solution.py
@@ -1,6 +1,10 @@
+import functools
+
 import jax
 import jax.numpy as jnp
 from jax import lax
+from jax.experimental import pallas as pl
+from jax.experimental.pallas import tpu as pltpu
 from jax.sharding import PartitionSpec as P
 
 
@@ -17,6 +21,175 @@
 
 def matvec(matrix, vector):
     return jnp.sum(matrix * vector[None, :], axis=1)
+
+
+def halves(value):
+    high = value.astype(jnp.bfloat16)
+    return high, (value - high.astype(jnp.float32)).astype(jnp.bfloat16)
+
+
+def three_pass(left, right, across):
+    dims = (((1,), (across,)), ((), ()))
+    left_high, left_low = halves(left)
+    right_high, right_low = halves(right)
+
+    def dot(a, b):
+        return lax.dot_general(a, b, dims, preferred_element_type=jnp.float32)
+
+    return dot(left_high, right_high) + (dot(left_high, right_low) + dot(left_low, right_high))
+
+
+def send_order(steps, hops):
+    order, reached, at = [], [0] * steps, [-2] * steps
+    while len(order) < steps * hops:
+        ready = [k for k in range(steps) if reached[k] < hops]
+        k = next((k for k in ready if at[k] <= len(order) - 2), ready[0])
+        order.append((k, reached[k]))
+        reached[k] += 1
+        at[k] = len(order) - 1
+    return order
+
+
+def block_kernel(
+    n, e_ref, g_ref, l_ref, whole_ref, gains_ref, covs_ref, cov_ref, offsets_ref,
+    columns_ref, pieces_ref, e_send, e_recv, z_send, z_recv, c_send, c_recv, g_send, g_recv,
+):
+    steps, rows, width = e_ref.shape
+    me = lax.axis_index("panel")
+    right = lax.rem(me + 1, n)
+    peers = [lax.rem(me + d, n) for d in range(1, n)]
+
+    def part(owner):
+        return pl.ds(pl.multiple_of(owner * rows, rows), rows)
+
+    def copy(source, target, send_sem, recv_sem, peer):
+        return pltpu.make_async_remote_copy(
+            src_ref=source, dst_ref=target, send_sem=send_sem, recv_sem=recv_sem,
+            device_id={"panel": peer}, device_id_type=pl.DeviceIdType.MESH,
+        )
+
+    barrier = pltpu.get_barrier_semaphore()
+    for peer in peers:
+        pl.semaphore_signal(
+            barrier, inc=1, device_id={"panel": peer}, device_id_type=pl.DeviceIdType.MESH
+        )
+    pl.semaphore_wait(barrier, n - 1)
+
+    arrival = [steps - 2, steps - 1, *range(steps - 3, -1, -1)]
+    order = [(arrival[k], hop) for k, hop in send_order(steps, n - 1)]
+    ring, landed, sent = {}, set(), []
+
+    def land(k, hop):
+        if (k, hop) not in landed:
+            ring[k, hop].wait_recv()
+            landed.add((k, hop))
+
+    def pump(count):
+        for _ in range(min(count, len(order) - len(ring))):
+            k, hop = order[len(ring)]
+            owner = lax.rem(me - hop + n, n)
+            if hop > 0:
+                land(k, hop - 1)
+            source = e_ref.at[k] if hop == 0 else whole_ref.at[k, part(owner)]
+            ring[k, hop] = copy(
+                source, whole_ref.at[k, part(owner)], e_send.at[k, hop], e_recv.at[k, hop], right
+            )
+            ring[k, hop].start()
+
+    def complete(k):
+        while (k, n - 2) not in ring:
+            pump(1)
+        land(k, n - 2)
+
+    pump(2)
+    for d, peer in enumerate(peers):
+        small = copy(g_ref, offsets_ref.at[me], g_send.at[d], g_recv.at[d], peer)
+        small.start()
+        sent.append(small)
+    smalls = list(sent)
+    offsets_ref[me] = g_ref[...]
+    for k in range(steps):
+        whole_ref[k, part(me)] = e_ref[k]
+    covs_ref[steps - 1] = l_ref[steps - 1]
+
+    def compose(k):
+        @pl.loop(0, width // 128)
+        def _(tile):
+            at = pl.ds(pl.multiple_of(tile * 128, 128), 128)
+            after = whole_ref[steps - 1] if k == steps - 2 else gains_ref[k + 1]
+            gains_ref[k, at] = three_pass(whole_ref[k, at], after, 0)
+
+    for k in range(steps - 2, -1, -1):
+        complete(k)
+        pump(2)
+        columns_ref[k] = three_pass(whole_ref[k], covs_ref[k + 1], 1)
+        swaps = []
+        for d, peer in enumerate(peers):
+            swap = copy(
+                columns_ref.at[k, part(peer)], pieces_ref.at[k, me],
+                z_send.at[k, d], z_recv.at[k, d], peer,
+            )
+            swap.start()
+            swaps.append(swap)
+        pieces_ref[k, me] = columns_ref[k, part(me)]
+        if k == steps - 2:
+            complete(steps - 1)
+            pump(1)
+        if k > 0:
+            compose(k)
+        for swap in swaps:
+            swap.wait_recv()
+        sent.extend(swaps)
+        pieces = jnp.concatenate([pieces_ref[k, p] for p in range(n)], axis=1)
+        covs_ref[k] = three_pass(pieces, whole_ref[k], 1) + l_ref[k]
+
+    cov_ref[part(me)] = covs_ref[0]
+    for hop in range(n - 1):
+        owner = lax.rem(me - hop + n, n)
+        source = covs_ref.at[0] if hop == 0 else cov_ref.at[part(owner)]
+        move = copy(source, cov_ref.at[part(owner)], c_send.at[hop], c_recv.at[hop], right)
+        move.start()
+        if hop == 0:
+            compose(0)
+        move.wait_recv()
+        sent.append(move)
+    for small in smalls:
+        small.wait_recv()
+    for move in [*ring.values(), *sent]:
+        move.wait_send()
+
+
+def block_element(transitions, offsets, noise_cov):
+    steps, rows, width = transitions.shape
+    n = lax.axis_size("panel")
+    f32 = jnp.float32
+    vmem = pl.BlockSpec(memory_space=pltpu.VMEM)
+    dma = pltpu.SemaphoreType.DMA
+    return pl.pallas_call(
+        functools.partial(block_kernel, n),
+        out_shape=(
+            jax.ShapeDtypeStruct((steps, width, width), f32),
+            jax.ShapeDtypeStruct((steps - 1, width, width), f32),
+            jax.ShapeDtypeStruct((steps, rows, width), f32),
+            jax.ShapeDtypeStruct((width, width), f32),
+            jax.ShapeDtypeStruct((n, steps, rows), f32),
+        ),
+        in_specs=[vmem] * 3,
+        out_specs=(vmem,) * 5,
+        scratch_shapes=[
+            pltpu.VMEM((steps - 1, width, rows), f32),
+            pltpu.VMEM((steps - 1, n, rows, rows), f32),
+            dma((steps, n - 1)), dma((steps, n - 1)),
+            dma((steps - 1, n - 1)), dma((steps - 1, n - 1)),
+            dma((n - 1,)), dma((n - 1,)), dma((n - 1,)), dma((n - 1,)),
+        ],
+        compiler_params=pltpu.CompilerParams(
+            collective_id=0, has_side_effects=True, vmem_limit_bytes=48 * 2**20
+        ),
+        cost_estimate=pl.CostEstimate(
+            flops=18 * width**3, bytes_accessed=12 * 2**20, transcendentals=0
+        ),
+    )(transitions, offsets, noise_cov)
 
 
 def send(value, pairs):
@@ -82,24 +255,36 @@
 def per_device(transitions, offsets, noise_cov):
     steps, rows = transitions.shape[:2]
     start = lax.axis_index("panel") * rows
-    whole = {}
-    for k in [*range(steps - 2, -1, -1), steps - 1]:
-        whole[k] = lax.all_gather(transitions[k], "panel", axis=0, tiled=True)
-    all_offsets = lax.all_gather(offsets, "panel", axis=1, tiled=True)
-    cov = noise_cov[steps - 1]
-    offset = all_offsets[steps - 1]
-    gain = whole[steps - 1]
-    covs, gains, means = [cov], [gain], [offset]
-    for k in range(steps - 2, -1, -1):
-        columns = product_t(whole[k], cov)
-        mine = lax.all_to_all(columns, "panel", split_axis=0, concat_axis=1, tiled=True)
-        cov = product_t(mine, whole[k]) + noise_cov[k]
-        gain = product(whole[k], gain)
-        offset = matvec(whole[k], offset) + all_offsets[k]
-        covs.append(cov)
-        gains.append(gain)
-        means.append(offset)
-    whole_cov = lax.all_gather(cov, "panel", axis=0, tiled=True)
+    if rows % 128 == 0 and steps > 1:
+        whole, composed, covs, whole_cov, parts = block_element(
+            transitions, offsets, noise_cov
+        )
+        all_offsets = jnp.swapaxes(parts, 0, 1).reshape(steps, -1)
+        gains = [whole[steps - 1], *(composed[k] for k in range(steps - 2, -1, -1))]
+        means = [all_offsets[steps - 1]]
+        for k in range(steps - 2, -1, -1):
+            means.append(matvec(whole[k], means[-1]) + all_offsets[k])
+        covs = [covs[k] for k in range(steps - 1, -1, -1)]
+        gain, offset = gains[-1], means[-1]
+    else:
+        whole = {}
+        for k in [*range(steps - 2, -1, -1), steps - 1]:
+            whole[k] = lax.all_gather(transitions[k], "panel", axis=0, tiled=True)
+        all_offsets = lax.all_gather(offsets, "panel", axis=1, tiled=True)
+        cov = noise_cov[steps - 1]
+        offset = all_offsets[steps - 1]
+        gain = whole[steps - 1]
+        covs, gains, means = [cov], [gain], [offset]
+        for k in range(steps - 2, -1, -1):
+            columns = product_t(whole[k], cov)
+            mine = lax.all_to_all(columns, "panel", split_axis=0, concat_axis=1, tiled=True)
+            cov = product_t(mine, whole[k]) + noise_cov[k]
+            gain = product(whole[k], gain)
+            offset = matvec(whole[k], offset) + all_offsets[k]
+            covs.append(cov)
+            gains.append(gain)
+            means.append(offset)
+        whole_cov = lax.all_gather(cov, "panel", axis=0, tiled=True)
     next_mean, next_cov = later_state(gain, offset, whole_cov)
     covs, gains, means = covs[::-1], gains[::-1], means[::-1]
     own = jnp.concatenate([lax.dynamic_slice_in_dim(f, start, rows, 0) for f in gains])

time: 263 us -> 220 us (0.84)
  Pallas kernels: 0 us -> 137 us
  waiting for transfers between devices: 140 us -> 23.9 us
  blocking collectives: 21.4 us -> 0 us
  matrix products: 42.3 us -> 22.9 us
  between operations: 14.4 us -> 1.1 us
  starting transfers between devices: 20.8 us -> 11.2 us
  other arithmetic: 1.81 us -> 8.41 us
  local copies, waits for them, and re-layouts: 19.9 us -> 13.9 us
    pallas_call x0 -> x1, Pallas kernels: none -> 137 us  [block_element(): pl.pallas_call(functools.partial(block_kernel, n), out_shape=(jax.ShapeDt...]
    all_gather x5 -> x0, waiting for transfers between devices: 93.2 us -> none  [the longest x4 70 us: per_device(): whole[k] = lax.all_gather(transitions[k], 'panel', axis=0, tiled=True)]
    all_gather x1 -> x0, blocking collectives: 21.4 us -> none  [per_device(): all_offsets = lax.all_gather(offsets, 'panel', axis=1, tiled=True)]
    all_to_all x3 -> x0, waiting for transfers between devices: 12.5 us -> none  [per_device(): lax.all_to_all(columns, 'panel', split_axis=0, concat_axis=1, tiled=True)]
    all_to_all x3 -> x0, starting transfers between devices: 10.9 us -> none  [per_device(): lax.all_to_all(columns, 'panel', split_axis=0, concat_axis=1, tiled=True)]
    dot_general x10 -> x7, matrix products: 25.4 us -> 14.7 us  [product(): jnp.dot(left, right, precision=lax.Precision.HIGH, preferred_element_type...]
    ppermute x15, waiting for transfers between devices: 32.8 us -> 23.9 us  [send(): return lax.ppermute(value, 'tm', pairs)]
    dot_general x14 -> x8, matrix products: 16.9 us -> 8.16 us  [product_t(): lax.dot_general(left, right, (((1,), (1,)), ((), ())), precision=lax.Prec...]
  transfers between devices with their start and end apart: 23 -> 15, of which waited for: 12 -> 6; matrix products, arithmetic and copies ran while one was open for 16% -> 13% of each run, Pallas kernels for 0% -> 0%
where the time goes in v2:
time: 220 us; the launch traced here: 219 us
  Pallas kernels  137 us (62%)
  waiting for transfers between devices  23.9 us (11%)
  matrix products  22.9 us (10%)
  local copies, waits for them, and re-layouts  13.9 us (6%)
  starting transfers between devices  11.2 us (5%)
  other arithmetic  8.41 us (4%)
    pallas_call x1, Pallas kernels, block_element(): pl.pallas_call(functools.partial(block_kernel, n), out_shape=(jax.ShapeDt...  137 us
    ppermute x15, waiting for transfers between devices, send(): return lax.ppermute(value, 'tm', pairs)  23.9 us
    dot_general x7, matrix products, product(): jnp.dot(left, right, precision=lax.Precision.HIGH, preferred_element_type...  14.7 us
    ppermute x15, starting transfers between devices, send(): return lax.ppermute(value, 'tm', pairs)  11.2 us
    dot_general x8, matrix products, product_t(): lax.dot_general(left, right, (((1,), (1,)), ((), ())), precision=lax.Prec...  8.16 us
  transfers between devices with their start and end apart: 15, of which 6 were waited for; matrix products, arithmetic and copies ran while one was open for 13% of the time, Pallas kernels for 0%

profile of v2, /device:TPU:0, one launch (start us, length us, event | category | flops | bytes accessed | tf_op | source)
XLA Modules:
  0.0 218.8 jit_solution(2638286900093393135)
XLA Ops:
  0.6 1.2 copy-done
  1.9 1.2 copy-done.1
  3.1 0.7 copy-done.2
  3.8 137.3 %shard_map.50 = (f32[4,512,512]{2,1,0:T(8,128)}, f32[3,512,512]{2,1,0:T(8,128)}, f32[4,128,512]{2,1,0:T(8,128)S(1)}, f32[512,512]{1,0:T(8,128)S(1)}, f32[4,4,128]{2,1,0:T(4,128)S(1)}) custom-call(f32[4,128,512]{2,1,0:T(8,128)S(1)} %copy-done, f32[4,128]{1,0:T(4,128)S(1)} %copy-done.2, f32[4,128,512]{2,1,0:T(8,128)S(1)} %copy-done.1), custom_call_target="tpu_custom_call" | custom-call | flops 2415919104 | bytes 12582912 | tf_op jit(solution)/shard_map/pallas_call | solution.py:168
  141.1 4.3 %slice_bitcast_fusion = (f32[512,512]{1,0:T(8,128)}, f32[1,512,512]{2,1,0:T(8,128)}, f32[1,512,512]{2,1,0:T(8,128)}, f32[1,512,512]{2,1,0:T(8,128)}) fusion(f32[3,512,512]{2,1,0:T(8,128)} %get-tuple-element.7), kind=kLoop, calls=%fused_computation.104 | loop fusion | bytes 7340032 | tf_op jit(solution)/shard_map/squeeze | solution.py:263
  145.4 0.0 collective-permute-start
  145.4 0.2 fusion.19
  145.6 0.2 fusion.20
  145.7 0.2 fusion.21
  145.9 0.6 collective-permute-start.3
  146.5 0.1 collective-permute-start.9
  146.5 1.0 slice.98
  147.6 1.8 dynamic-slice_bitcast_fusion
  149.3 1.9 dynamic-slice_bitcast_fusion.2
  151.2 1.4 multiply_reduce_fusion.4
  152.6 1.6 collective-permute-start.4
  154.2 2.6 %fusion.23 = f32[512,512]{1,0:T(8,128)S(1)} fusion(f32[512,512]{1,0:T(8,128)} %collective-permute-done.9, f32[512,512]{1,0:T(8,128)S(1)} %get-tuple-element.10, pred[]{:T(512)S(6)} %eq.14, f32[512,512]{1,0:T(8,128)S(1)} %collective-permute-done, f32[3,512,512]{2,1,0:T(8,128)} %get-tuple-element.7), kind=kOutput, calls=%fused_computation.40 | convolution fusion | flops 805830656 | bytes 5243904 | tf_op jit(solution)/shard_map/dot_general | solution.py:12
  156.8 1.1 convolution_add_fusion.1
  158.0 1.0 slice_select_fusion.1
  158.9 0.2 copy-done.5
  159.2 1.3 collective-permute-start.10
  160.4 1.1 fusion.25
  161.6 1.3 copy.5
  162.9 0.0 collective-permute-done.4
  162.9 1.3 collective-permute-start.5
  164.2 2.1 slice_select_fusion.2
  166.3 1.3 collective-permute-start.1
  167.6 8.3 %collective-permute-done.10 = f32[256,512]{1,0:T(8,128)} collective-permute-done((f32[256,512]{1,0:T(8,128)}, f32[256,512]{1,0:T(8,128)}, u32[]{:S(2)}, u32[]{:S(2)}) %collective-permute-start.10) | collective-permute-done | bytes 524320 | tf_op jit(solution)/shard_map/ppermute | solution.py:196
  175.9 0.7 collective-permute-start.11
  176.6 1.5 multiply_reduce_fusion.1
  178.1 1.3 collective-permute-start.6
  179.4 0.8 collective-permute-start.7
  180.3 3.3 %collective-permute-done.6 = f32[256]{0:T(256)S(1)} collective-permute-done((f32[256]{0:T(256)S(1)}, f32[256]{0:T(256)S(1)}, u32[]{:S(2)}, u32[]{:S(2)}) %collective-permute-start.6) | collective-permute-done | bytes 1056 | tf_op jit(solution)/shard_map/ppermute | solution.py:196
  183.5 0.0 collective-permute-done.7
  183.5 0.0 collective-permute-start.8
  183.6 0.1 dynamic_slice.43
  183.7 0.1 dynamic_slice.42
  183.7 0.1 dynamic_slice.41
  183.8 0.1 dynamic_slice.40
  183.9 0.8 collective-permute-done.8
  184.7 2.4 %collective-permute-done.1 = f32[256,512]{1,0:T(8,128)} collective-permute-done((f32[256,512]{1,0:T(8,128)}, f32[256,512]{1,0:T(8,128)}, u32[]{:S(2)}, u32[]{:S(2)}) %collective-permute-start.1) | collective-permute-done | bytes 524320 | tf_op jit(solution)/shard_map/ppermute | solution.py:196
  187.1 0.1 collective-permute-start.2
  187.2 2.5 %fusion.29 = f32[512,512]{1,0:T(8,128)S(1)} fusion(f32[512,512]{0,1:T(8,128)S(1)} %fusion.25, f32[256,512]{1,0:T(8,128)} %collective-permute-done.11, f32[256,512]{1,0:T(8,128)} %collective-permute-done.10, pred[]{:T(512)S(6)} %eq.14), kind=kOutput, calls=%fused_computation.53 | convolution fusion | flops 806092800 | bytes 3145729 | tf_op jit(solution)/shard_map/dot_general | solution.py:12
  189.8 1.0 convolution_add_fusion
  190.8 0.1 slice_select_fusion
  190.9 1.4 collective-permute-start.12
  192.3 0.7 collective-permute-start.13
  193.1 2.5 %multiply_reduce_fusion.2 = (f32[512]{0:T(512)S(1)}, f32[512,512]{1,0:T(8,128)S(1)}) fusion(f32[512]{0:T(512)S(1)} %maximum_select_fusion.8, f32[512,512]{1,0:T(8,128)S(1)} %collective-permute-done, pred[]{:T(512)S(6)} %eq.14, f32[256,512]{1,0:T(8,128)S(1)} %collective-permute-done.2, f32[256,512]{1,0:T(8,128)} %collective-permute-done.1, pred[]{:T(512)S(6)} %eq.13), kind=kOutput, calls=%fused_computation.44 | convolution fusion | flops 808451584 | bytes 3149826 | tf_op jit(solution)/shard_map/dot_general | solution.py:12
  195.6 0.2 multiply_reduce_fusion
  195.7 2.5 %fusion.27 = f32[512,512]{1,0:T(8,128)S(1)} fusion(f32[512,512]{1,0:T(8,128)S(1)} %collective-permute-done, f32[256,512]{1,0:T(8,128)} %collective-permute-done.11, f32[256,512]{1,0:T(8,128)} %collective-permute-done.10, pred[]{:T(512)S(6)} %eq.14), kind=kOutput, calls=%fused_computation.51 | convolution fusion | flops 806879232 | bytes 3145729 | tf_op jit(solution)/shard_map/dot_general | solution.py:12
  198.3 8.9 %collective-permute-done.12 = f32[256,512]{1,0:T(8,128)S(1)} collective-permute-done((f32[256,512]{1,0:T(8,128)S(1)}, f32[256,512]{1,0:T(8,128)S(1)}, u32[]{:S(2)}, u32[]{:S(2)}) %collective-permute-start.12) | collective-permute-done | bytes 524320 | tf_op jit(solution)/shard_map/ppermute | solution.py:196
  207.2 0.1 add.104
  207.3 0.1 collective-permute-start.14
  207.3 0.6 fusion.45
  207.9 1.0 fusion.28
  209.0 0.3 collective-permute-done.14
  209.2 1.0 fusion.10
  210.3 1.1 fusion.64
  211.3 2.5 %fusion.4 = f32[512,512]{1,0:T(8,128)S(1)} fusion(f32[512,512]{1,0:T(8,128)S(1)} %fusion.64, f32[512,512]{1,0:T(8,128)S(1)} %fusion.28, f32[512,512]{1,0:T(8,128)} %collective-permute-done.9, f32[128,512]{1,0:T(8,128)S(1)} %get-tuple-element.24, f32[128,512]{1,0:T(8,128)S(1)} %copy-done.8, f32[128,512]{1,0:T(8,128)S(1)} %copy-done.9, ...), kind=kOutput, calls=%fused_computation.13 | convolution fusion | flops 807403520 | bytes 5242883 | tf_op jit(solution)/shard_map/dot_general | solution.py:12
  213.8 1.9 fusion
  215.7 0.7 fusion.1
  216.4 0.7 fusion.2
  217.1 0.7 fusion.3
  217.8 1.0 pad_maximum_fusion.1
  (38 shorter events, 0.1 us)
Async XLA Ops:
  0.6 1.2 copy-start
  1.9 1.2 copy-start.1
  3.1 0.7 copy-start.2
  141.1 4.3 %copy-start.7 = (f32[4,512,512]{2,1,0:T(8,128)S(1)}, f32[4,512,512]{2,1,0:T(8,128)}, u32[]{:S(2)}) copy-start(f32[4,512,512]{2,1,0:T(8,128)} %get-tuple-element.8) | copy-start | bytes 12582916
  145.4 5.8 %collective-permute-start = (f32[512,512]{1,0:T(8,128)}, f32[512,512]{1,0:T(8,128)S(1)}, u32[]{:S(2)}, u32[]{:S(2)}) collective-permute-start(f32[512,512]{1,0:T(8,128)} %get-tuple-element.14), channel_id=1, source_target_pairs={{0,4},{4,0},{8,12},{12,8},{16,20},{20,16},{24,28},{28,24},{1,5},{5... | collective-permute-start | bytes 3145736 | tf_op jit(solution)/shard_map/ppermute | solution.py:196
  145.9 5.3 %collective-permute-start.3 = (f32[512]{0:T(512)S(1)}, f32[512]{0:T(512)S(1)}, u32[]{:S(2)}, u32[]{:S(2)}) collective-permute-start(f32[512]{0:T(512)S(1)} %add.94), channel_id=1, source_target_pairs={{0,4},{4,0},{8,12},{12,8},{16,20},{20,16},{24,28},{28,24},{1,5},{5... | collective-permute-start | bytes 6152 | tf_op jit(solution)/shard_map/ppermute | solution.py:196
  146.5 7.8 %collective-permute-start.9 = (f32[512,512]{1,0:T(8,128)S(1)}, f32[512,512]{1,0:T(8,128)}, u32[]{:S(2)}, u32[]{:S(2)}) collective-permute-start(f32[512,512]{1,0:T(8,128)S(1)} %get-tuple-element.10), channel_id=1, source_target_pairs={{0,4},{4,0},{8,12},{12,8},{16,20},{20,16},{24,28},{28,24},{1,5},{5... | collective-permute-start | bytes 3145736 | tf_op jit(solution)/shard_map/ppermute | solution.py:196
  152.6 4.2 %copy-start.3 = (f32[3,512,512]{2,1,0:T(8,128)S(1)}, f32[3,512,512]{2,1,0:T(8,128)}, u32[]{:S(2)}) copy-start(f32[3,512,512]{2,1,0:T(8,128)} %get-tuple-element.7) | copy-start | bytes 9437188
  152.6 10.2 %collective-permute-start.4 = (f32[256]{0:T(256)S(1)}, f32[256]{0:T(256)S(1)}, u32[]{:S(2)}, u32[]{:S(2)}) collective-permute-start(f32[256]{0:T(256)S(1)} %slice_select_fusion.4), channel_id=1, source_target_pairs={{8,0},{12,4},{24,16},{28,20},{9,1},{13,5},{25,17},{29,21},{10,2},{... | collective-permute-start | bytes 3080 | tf_op jit(solution)/shard_map/ppermute | solution.py:196
  158.0 1.2 copy-start.5
  159.2 16.7 %collective-permute-start.10 = (f32[256,512]{1,0:T(8,128)}, f32[256,512]{1,0:T(8,128)}, u32[]{:S(2)}, u32[]{:S(2)}) collective-permute-start(f32[256,512]{1,0:T(8,128)} %slice_select_fusion.1), channel_id=1, source_target_pairs={{8,0},{12,4},{24,16},{28,20},{9,1},{13,5},{25,17},{29,21},{10,2},{... | collective-permute-start | bytes 1572872 | tf_op jit(solution)/shard_map/ppermute | solution.py:196
  162.9 4.7 %collective-permute-start.5 = (f32[256]{0:T(256)S(1)}, f32[256]{0:T(256)S(1)}, u32[]{:S(2)}, u32[]{:S(2)}) collective-permute-start(f32[256]{0:T(256)S(1)} %collective-permute-done.4), channel_id=1, source_target_pairs={{0,4},{4,0},{8,12},{12,8},{16,20},{20,16},{24,28},{28,24},{1,5},{5... | collective-permute-start | bytes 3080 | tf_op jit(solution)/shard_map/ppermute | solution.py:196
  166.3 20.8 %collective-permute-start.1 = (f32[256,512]{1,0:T(8,128)}, f32[256,512]{1,0:T(8,128)}, u32[]{:S(2)}, u32[]{:S(2)}) collective-permute-start(f32[256,512]{1,0:T(8,128)} %slice_select_fusion.2), channel_id=1, source_target_pairs={{8,0},{12,4},{9,1},{13,5},{10,2},{14,6},{11,3},{15,7}} | collective-permute-start | bytes 1572872 | tf_op jit(solution)/shard_map/ppermute | solution.py:196
  175.9 11.4 %collective-permute-start.11 = (f32[256,512]{1,0:T(8,128)}, f32[256,512]{1,0:T(8,128)}, u32[]{:S(2)}, u32[]{:S(2)}) collective-permute-start(f32[256,512]{1,0:T(8,128)} %collective-permute-done.10), channel_id=1, source_target_pairs={{0,4},{4,0},{8,12},{12,8},{16,20},{20,16},{24,28},{28,24},{1,5},{5... | collective-permute-start | bytes 1572872 | tf_op jit(solution)/shard_map/ppermute | solution.py:196
  178.1 5.5 %collective-permute-start.6 = (f32[256]{0:T(256)S(1)}, f32[256]{0:T(256)S(1)}, u32[]{:S(2)}, u32[]{:S(2)}) collective-permute-start(f32[256]{0:T(256)S(1)} %slice_select_fusion.3), channel_id=1, source_target_pairs={{16,0},{20,4},{17,1},{21,5},{18,2},{22,6},{19,3},{23,7}} | collective-permute-start | bytes 3080 | tf_op jit(solution)/shard_map/ppermute | solution.py:196
  179.4 4.2 %collective-permute-start.7 = (f32[256]{0:T(256)S(1)}, f32[256]{0:T(256)S(1)}, u32[]{:S(2)}, u32[]{:S(2)}) collective-permute-start(f32[256]{0:T(256)S(1)} %slice_select_fusion.3), channel_id=1, source_target_pairs={{16,8},{20,12},{17,9},{21,13},{18,10},{22,14},{19,11},{23,15}} | collective-permute-start | bytes 3080 | tf_op jit(solution)/shard_map/ppermute | solution.py:196
  183.5 1.1 collective-permute-start.8
  183.9 5.9 %copy-start.6 = (f32[512,512]{1,0:T(8,128)S(1)}, f32[512,512]{1,0:T(8,128)}, u32[]{:S(2)}) copy-start(f32[512,512]{1,0:T(8,128)} %copy-done.5) | copy-start | bytes 3145732
  187.1 6.0 %collective-permute-start.2 = (f32[256,512]{1,0:T(8,128)}, f32[256,512]{1,0:T(8,128)S(1)}, u32[]{:S(2)}, u32[]{:S(2)}) collective-permute-start(f32[256,512]{1,0:T(8,128)} %collective-permute-done.1), channel_id=1, source_target_pairs={{0,4},{4,0},{8,12},{12,8},{16,20},{20,16},{24,28},{28,24},{1,5},{5... | collective-permute-start | bytes 1572872 | tf_op jit(solution)/shard_map/ppermute | solution.py:196
  190.8 4.8 %copy-start.8 = (f32[128,512]{1,0:T(8,128)S(1)}, f32[128,512]{1,0:T(8,128)}, u32[]{:S(2)}) copy-start(f32[128,512]{1,0:T(8,128)} %get-tuple-element.25) | copy-start | bytes 786436
  190.8 4.8 %copy-start.9 = (f32[128,512]{1,0:T(8,128)S(1)}, f32[128,512]{1,0:T(8,128)}, u32[]{:S(2)}) copy-start(f32[128,512]{1,0:T(8,128)} %get-tuple-element.26) | copy-start | bytes 786436
  190.8 4.8 %copy-start.10 = (f32[128,512]{1,0:T(8,128)S(1)}, f32[128,512]{1,0:T(8,128)}, u32[]{:S(2)}) copy-start(f32[128,512]{1,0:T(8,128)} %get-tuple-element.27) | copy-start | bytes 786436
  190.9 16.2 %collective-permute-start.12 = (f32[256,512]{1,0:T(8,128)S(1)}, f32[256,512]{1,0:T(8,128)S(1)}, u32[]{:S(2)}, u32[]{:S(2)}) collective-permute-start(f32[256,512]{1,0:T(8,128)S(1)} %slice_select_fusion), channel_id=1, source_target_pairs={{16,0},{20,4},{17,1},{21,5},{18,2},{22,6},{19,3},{23,7}} | collective-permute-start | bytes 1572872 | tf_op jit(solution)/shard_map/ppermute | solution.py:196
  192.3 14.8 %collective-permute-start.13 = (f32[256,512]{1,0:T(8,128)S(1)}, f32[256,512]{1,0:T(8,128)S(1)}, u32[]{:S(2)}, u32[]{:S(2)}) collective-permute-start(f32[256,512]{1,0:T(8,128)S(1)} %slice_select_fusion), channel_id=1, source_target_pairs={{16,8},{20,12},{17,9},{21,13},{18,10},{22,14},{19,11},{23,15}} | collective-permute-start | bytes 1572872 | tf_op jit(solution)/shard_map/ppermute | solution.py:196
  207.3 2.0 collective-permute-start.14
  211.3 4.4 %copy-start.4 = (f32[3,512,512]{2,1,0:T(8,128)S(1)}, f32[3,512,512]{2,1,0:T(8,128)}, u32[]{:S(2)}) copy-start(f32[3,512,512]{2,1,0:T(8,128)} %get-tuple-element.7) | copy-start | bytes 9437188

commit v3 on v2

--- a/solution.py
+++ b/solution.py
@@ -51,10 +51,12 @@
 
 
 def block_kernel(
-    n, e_ref, g_ref, l_ref, whole_ref, gains_ref, covs_ref, cov_ref, offsets_ref,
-    columns_ref, pieces_ref, e_send, e_recv, z_send, z_recv, c_send, c_recv, g_send, g_recv,
+    n, e_ref, g_ref, l_ref, whole_ref, own_ref, covs_ref, cov_ref, offsets_ref, *more
 ):
     steps, rows, width = e_ref.shape
+    gains = more[: steps - 1]
+    (columns_ref, pieces_ref, e_send, e_recv, z_send, z_recv, c_send, c_recv, g_send,
+     g_recv) = more[steps - 1 :]
     me = lax.axis_index("panel")
     right = lax.rem(me + 1, n)
     peers = [lax.rem(me + d, n) for d in range(1, n)]
@@ -116,8 +118,8 @@
         @pl.loop(0, width // 128)
         def _(tile):
             at = pl.ds(pl.multiple_of(tile * 128, 128), 128)
-            after = whole_ref[steps - 1] if k == steps - 2 else gains_ref[k + 1]
-            gains_ref[k, at] = three_pass(whole_ref[k, at], after, 0)
+            after = whole_ref[steps - 1] if k == steps - 2 else gains[k + 1][...]
+            gains[k][at] = three_pass(whole_ref[k, at], after, 0)
 
     for k in range(steps - 2, -1, -1):
         complete(k)
@@ -143,16 +145,35 @@
         pieces = jnp.concatenate([pieces_ref[k, p] for p in range(n)], axis=1)
         covs_ref[k] = three_pass(pieces, whole_ref[k], 1) + l_ref[k]
 
-    cov_ref[part(me)] = covs_ref[0]
+    kept = n // 2 + 1
+    for j in range(kept):
+        at = part(lax.rem(me + j, n))
+        cov_ref[part(me), at] = covs_ref[0, :, at]
     for hop in range(n - 1):
         owner = lax.rem(me - hop + n, n)
-        source = covs_ref.at[0] if hop == 0 else cov_ref.at[part(owner)]
-        move = copy(source, cov_ref.at[part(owner)], c_send.at[hop], c_recv.at[hop], right)
-        move.start()
+        moves = []
+        for j in range(kept):
+            at = part(lax.rem(owner + j, n))
+            source = covs_ref.at[0, :, at] if hop == 0 else cov_ref.at[part(owner), at]
+            move = copy(
+                source, cov_ref.at[part(owner), at], c_send.at[hop, j], c_recv.at[hop, j], right
+            )
+            move.start()
+            moves.append(move)
         if hop == 0:
             compose(0)
-        move.wait_recv()
-        sent.append(move)
+        for move in moves:
+            move.wait_recv()
+        sent.extend(moves)
+    for p in range(n):
+        for j in range(kept, n):
+            q = (p + j) % n
+            cov_ref[p * rows : (p + 1) * rows, q * rows : (q + 1) * rows] = cov_ref[
+                q * rows : (q + 1) * rows, p * rows : (p + 1) * rows
+            ].T
+    own_ref[steps - 1] = e_ref[steps - 1]
+    for k in range(steps - 1):
+        own_ref[k] = gains[k][part(me)]
     for small in smalls:
         small.wait_recv()
     for move in [*ring.values(), *sent]:
@@ -169,19 +190,20 @@
         functools.partial(block_kernel, n),
         out_shape=(
             jax.ShapeDtypeStruct((steps, width, width), f32),
-            jax.ShapeDtypeStruct((steps - 1, width, width), f32),
+            jax.ShapeDtypeStruct((steps, rows, width), f32),
             jax.ShapeDtypeStruct((steps, rows, width), f32),
             jax.ShapeDtypeStruct((width, width), f32),
             jax.ShapeDtypeStruct((n, steps, rows), f32),
+            *[jax.ShapeDtypeStruct((width, width), f32)] * (steps - 1),
         ),
         in_specs=[vmem] * 3,
-        out_specs=(vmem,) * 5,
+        out_specs=(vmem,) * (steps + 4),
         scratch_shapes=[
             pltpu.VMEM((steps - 1, width, rows), f32),
             pltpu.VMEM((steps - 1, n, rows, rows), f32),
             dma((steps, n - 1)), dma((steps, n - 1)),
             dma((steps - 1, n - 1)), dma((steps - 1, n - 1)),
-            dma((n - 1,)), dma((n - 1,)), dma((n - 1,)), dma((n - 1,)),
+            dma((n - 1, n // 2 + 1)), dma((n - 1, n // 2 + 1)), dma((n - 1,)), dma((n - 1,)),
         ],
         compiler_params=pltpu.CompilerParams(
             collective_id=0, has_side_effects=True, vmem_limit_bytes=48 * 2**20
@@ -256,7 +278,7 @@
     steps, rows = transitions.shape[:2]
     start = lax.axis_index("panel") * rows
     if rows % 128 == 0 and steps > 1:
-        whole, composed, covs, whole_cov, parts = block_element(
+        whole, own, covs, whole_cov, parts, *composed = block_element(
             transitions, offsets, noise_cov
         )
         all_offsets = jnp.swapaxes(parts, 0, 1).reshape(steps, -1)
@@ -266,6 +288,7 @@
             means.append(matvec(whole[k], means[-1]) + all_offsets[k])
         covs = [covs[k] for k in range(steps - 1, -1, -1)]
         gain, offset = gains[-1], means[-1]
+        own = own.reshape(steps * rows, -1)
     else:
         whole = {}
         for k in [*range(steps - 2, -1, -1), steps - 1]:
@@ -285,9 +308,11 @@
             gains.append(gain)
             means.append(offset)
         whole_cov = lax.all_gather(cov, "panel", axis=0, tiled=True)
+        own = jnp.concatenate(
+            [lax.dynamic_slice_in_dim(f, start, rows, 0) for f in gains[::-1]]
+        )
     next_mean, next_cov = later_state(gain, offset, whole_cov)
     covs, gains, means = covs[::-1], gains[::-1], means[::-1]
-    own = jnp.concatenate([lax.dynamic_slice_in_dim(f, start, rows, 0) for f in gains])
     own_offsets = jnp.concatenate(
         [lax.dynamic_slice_in_dim(m, start, rows, 0) for m in means]
     )

time: 220 us -> 214 us (0.973)
  local copies, waits for them, and re-layouts: 13.9 us -> 4.47 us
  waiting for transfers between devices: 23.9 us -> 17.8 us
  matrix products: 22.9 us -> 27.2 us
  starting transfers between devices: 11.2 us -> 15 us
  other arithmetic: 8.41 us -> 11.2 us
    ppermute x15, waiting for transfers between devices: 23.9 us -> 17.8 us  [send(): return lax.ppermute(value, 'tm', pairs)]
    squeeze x1 -> x0, local copies, waits for them, and re-layouts: 4.25 us -> none  [per_device(): gains = [whole[steps - 1], *(composed[k] for k in range(steps - 2, -1, -1))]]
    ppermute x15, starting transfers between devices: 11.2 us -> 15 us  [send(): return lax.ppermute(value, 'tm', pairs)]
    dynamic_slice x2 -> x0, local copies, waits for them, and re-layouts: 3.62 us -> none  [per_device(): lax.dynamic_slice_in_dim(f, start, rows, 0)]
    reduce_sum x6, other arithmetic: 3.52 us -> 6.28 us  [matvec(): return jnp.sum(matrix * vector[None, :], axis=1)]
    dot_general x8, matrix products: 8.16 us -> 10.6 us  [product_t(): lax.dot_general(left, right, (((1,), (1,)), ((), ())), precision=lax.Prec...]
  transfers between devices with their start and end apart: 15 -> 15, of which waited for: 6 -> 6; matrix products, arithmetic and copies ran while one was open for 13% -> 14% of each run, Pallas kernels for 0% -> 0%
where the time goes in v3:
time: 214 us; the launch traced here: 213 us
  Pallas kernels  137 us (64%)
  matrix products  27.2 us (13%)
  waiting for transfers between devices  17.8 us (8%)
  starting transfers between devices  15 us (7%)
  other arithmetic  11.2 us (5%)
  local copies, waits for them, and re-layouts  4.47 us (2%)
    pallas_call x1, Pallas kernels, block_element(): pl.pallas_call(functools.partial(block_kernel, n), out_shape=(jax.ShapeDt...  137 us
    ppermute x15, waiting for transfers between devices, send(): return lax.ppermute(value, 'tm', pairs)  17.8 us
    dot_general x7, matrix products, product(): jnp.dot(left, right, precision=lax.Precision.HIGH, preferred_element_type...  16.6 us
    ppermute x15, starting transfers between devices, send(): return lax.ppermute(value, 'tm', pairs)  15 us
    dot_general x8, matrix products, product_t(): lax.dot_general(left, right, (((1,), (1,)), ((), ())), precision=lax.Prec...  10.6 us
    reduce_sum x6, other arithmetic, matvec(): return jnp.sum(matrix * vector[None, :], axis=1)  6.28 us
  transfers between devices with their start and end apart: 15, of which 6 were waited for; matrix products, arithmetic and copies ran while one was open for 14% of the time, Pallas kernels for 0%

profile of v3, /device:TPU:0, one launch (start us, length us, event | category | flops | bytes accessed | tf_op | source)
XLA Modules:
  0.0 213.2 jit_solution(6184313386819845946)
XLA Ops:
  0.6 0.7 copy-done.4
  1.3 136.5 %shard_map.50 = (f32[4,512,512]{2,1,0:T(8,128)}, f32[4,128,512]{2,1,0:T(8,128)S(1)}, f32[4,128,512]{2,1,0:T(8,128)S(1)}, f32[512,512]{1,0:T(8,128)S(1)}, f32[4,4...) custom-call(f32[4,128,512]{2,1,0:T(8,128)} %e_ref.1, ...), custom_call_target="tpu_custom_call" | custom-call | flops 2415919104 | bytes 12582912 | tf_op jit(solution)/shard_map/pallas_call | solution.py:189
  137.9 1.0 copy-done
  138.9 1.0 copy-done.2
  139.9 0.0 collective-permute-start
  139.9 0.5 collective-permute-start.9
  140.4 1.4 fusion.17
  141.8 1.4 fusion.18
  143.1 1.4 fusion.19
  144.5 0.1 collective-permute-start.3
  144.7 1.1 collective-permute-done.3
  145.8 0.0 collective-permute-done
  145.8 0.2 multiply_reduce_fusion.4
  146.0 1.3 collective-permute-start.4
  147.3 0.0 collective-permute-done.9
  147.3 2.3 %fusion.22 = f32[512,512]{1,0:T(8,128)S(1)} fusion(f32[512,512]{1,0:T(8,128)} %collective-permute-done.9, f32[512,512]{1,0:T(8,128)S(1)} %get-tuple-element.14, pred[]{:T(512)S(6)} %eq.14, f32[512,512]{1,0:T(8,128)S(1)} %get-tuple-element.11, f32[512,512]{1,0:T(8,128)} %collective-permute-done), kind=kOutput, calls=%fused_computation.38 | convolution fusion | flops 805830656 | bytes 5242881 | tf_op jit(solution)/shard_map/dot_general | solution.py:12
  149.6 1.1 convolution_add_fusion.1
  150.7 1.0 slice_select_fusion.1
  151.7 0.2 copy-done.5
  151.8 1.3 collective-permute-start.10
  153.1 2.3 %fusion.24 = f32[512,512]{0,1:T(8,128)S(1)} fusion(f32[512,512]{1,0:T(8,128)} %collective-permute-done, f32[512,512]{1,0:T(8,128)S(1)} %get-tuple-element.11, pred[]{:T(512)S(6)} %eq.14), kind=kOutput, calls=%fused_computation.45 | convolution fusion | flops 805830656 | bytes 3145729 | tf_op jit(solution)/shard_map/dot_general | solution.py:12
  155.4 1.3 copy.5
  156.7 0.0 collective-permute-done.4
  156.7 2.9 %collective-permute-start.5 = (f32[256]{0:T(256)S(1)}, f32[256]{0:T(256)S(1)}, u32[]{:S(2)}, u32[]{:S(2)}) collective-permute-start(f32[256]{0:T(256)S(1)} %collective-permute-done.4), channel_id=1, source_target_pairs={{0,4},{4,0},{8,12},{12,8},{16,20},{20,16},{24,28},{28,24},{1,5},{5... | collective-permute-start | bytes 3080 | tf_op jit(solution)/shard_map/ppermute | solution.py:218
  159.7 2.1 slice_select_fusion.2
  161.7 1.3 collective-permute-start.1
  163.0 0.0 collective-permute-done.5
  163.1 3.7 %collective-permute-done.10 = f32[256,512]{1,0:T(8,128)} collective-permute-done((f32[256,512]{1,0:T(8,128)}, f32[256,512]{1,0:T(8,128)}, u32[]{:S(2)}, u32[]{:S(2)}) %collective-permute-start.10) | collective-permute-done | bytes 524320 | tf_op jit(solution)/shard_map/ppermute | solution.py:218
  166.8 2.9 %collective-permute-start.11 = (f32[256,512]{1,0:T(8,128)}, f32[256,512]{1,0:T(8,128)}, u32[]{:S(2)}, u32[]{:S(2)}) collective-permute-start(f32[256,512]{1,0:T(8,128)} %collective-permute-done.10), channel_id=1, source_target_pairs={{0,4},{4,0},{8,12},{12,8},{16,20},{20,16},{24,28},{28,24},{1,5},{5... | collective-permute-start | bytes 1572872 | tf_op jit(solution)/shard_map/ppermute | solution.py:218
  169.7 1.8 multiply_reduce_fusion.1
  171.5 1.3 collective-permute-start.6
  172.8 0.8 collective-permute-start.7
  173.7 3.3 %collective-permute-done.6 = f32[256]{0:T(256)S(1)} collective-permute-done((f32[256]{0:T(256)S(1)}, f32[256]{0:T(256)S(1)}, u32[]{:S(2)}, u32[]{:S(2)}) %collective-permute-start.6) | collective-permute-done | bytes 1056 | tf_op jit(solution)/shard_map/ppermute | solution.py:218
  177.0 0.0 collective-permute-done.7
  177.0 0.1 dynamic_slice.15
  177.1 0.1 dynamic_slice.14
  177.1 0.1 dynamic_slice.13
  177.2 0.1 dynamic_slice.12
  177.3 0.8 collective-permute-done.8
  178.1 1.2 collective-permute-done.1
  179.3 0.5 collective-permute-start.2
  179.9 2.6 %fusion.28 = f32[512,512]{1,0:T(8,128)S(1)} fusion(f32[512,512]{0,1:T(8,128)S(1)} %fusion.24, f32[256,512]{1,0:T(8,128)} %collective-permute-done.11, f32[256,512]{1,0:T(8,128)} %collective-permute-done.10, pred[]{:T(512)S(6)} %eq.14), kind=kOutput, calls=%fused_computation.51 | convolution fusion | flops 806092800 | bytes 3145729 | tf_op jit(solution)/shard_map/dot_general | solution.py:12
  182.5 2.2 %convolution_add_fusion = f32[512,512]{1,0:T(8,128)S(1)} fusion(f32[512,512]{1,0:T(8,128)} %copy-done.5, f32[512,512]{1,0:T(8,128)S(1)} %fusion.28, f32[512,512]{0,1:T(8,128)S(1)} %fusion.24), kind=kOutput, calls=%fused_computation.3 | convolution fusion | flops 805568512 | bytes 4194304 | tf_op jit(solution)/shard_map/dot_general | solution.py:16
  184.8 0.1 slice_select_fusion
  184.8 1.3 collective-permute-start.12
  186.1 0.7 collective-permute-start.13
  186.9 3.0 %multiply_reduce_fusion.2 = (f32[512]{0:T(512)S(1)}, f32[512,512]{1,0:T(8,128)S(1)}) fusion(f32[512]{0:T(512)S(1)} %maximum_select_fusion.8, f32[512,512]{1,0:T(8,128)} %collective-permute-done, pred[]{:T(512)S(6)} %eq.14, f32[256,512]{1,0:T(8,128)S(1)} %collective-permute-done.2, f32[256,512]{1,0:T(8,128)} %collective-permute-done.1, pred[]{:T(512)S(6)} %eq.13), kind=kOutput, calls=%fused_computation.42 | convolution fusion | flops 808451584 | bytes 3149826 | tf_op jit(solution)/shard_map/dot_general | solution.py:12
  189.9 0.2 multiply_reduce_fusion
  190.1 2.9 %fusion.26 = f32[512,512]{1,0:T(8,128)S(1)} fusion(f32[512,512]{1,0:T(8,128)} %collective-permute-done, f32[256,512]{1,0:T(8,128)} %collective-permute-done.11, f32[256,512]{1,0:T(8,128)} %collective-permute-done.10, pred[]{:T(512)S(6)} %eq.14), kind=kOutput, calls=%fused_computation.49 | convolution fusion | flops 806879232 | bytes 3145729 | tf_op jit(solution)/shard_map/dot_general | solution.py:12
  192.9 7.6 %collective-permute-done.12 = f32[256,512]{1,0:T(8,128)S(1)} collective-permute-done((f32[256,512]{1,0:T(8,128)S(1)}, f32[256,512]{1,0:T(8,128)S(1)}, u32[]{:S(2)}, u32[]{:S(2)}) %collective-permute-start.12) | collective-permute-done | bytes 524320 | tf_op jit(solution)/shard_map/ppermute | solution.py:218
  200.6 0.0 collective-permute-done.13
  200.6 0.1 add.96
  200.7 0.1 collective-permute-start.14
  200.7 0.6 fusion.44
  201.3 2.3 %fusion.27 = f32[512,512]{1,0:T(8,128)S(1)} fusion(f32[512,512]{1,0:T(8,128)S(1)} %fusion.26, f32[512,512]{1,0:T(8,128)} %collective-permute-done, pred[]{:T(512)S(6)} %eq.14), kind=kOutput, calls=%fused_computation.50 | convolution fusion | flops 806092800 | bytes 3145729 | tf_op jit(solution)/shard_map/dot_general | solution.py:16
  203.6 0.0 collective-permute-done.14
  203.6 1.0 fusion.10
  204.7 1.1 fusion.51
  205.7 2.5 %fusion.4 = f32[512,512]{1,0:T(8,128)S(1)} fusion(f32[512,512]{1,0:T(8,128)S(1)} %bitcast.53, f32[512,512]{1,0:T(8,128)S(1)} %fusion.51, f32[512,512]{1,0:T(8,128)S(1)} %fusion.27, f32[512,512]{1,0:T(8,128)} %collective-permute-done.9, pred[]{:T(512)S(6)} %eq.12, pred[]{:T(512)S(6)} %eq.14, pred[]{:T(512)S(6)} %eq.13), kind=kOutput, calls=%fused_computation.13 | convolution fusion | flops 806617088 | bytes 5242883 | tf_op jit(solution)/shard_map/dot_general | solution.py:12
  208.3 1.9 fusion
  210.2 0.7 fusion.3
  210.8 0.7 fusion.1
  211.5 0.7 fusion.2
  212.2 1.0 pad_maximum_fusion
  (26 shorter events, 0.1 us)
Async XLA Ops:
  0.6 0.7 copy-start.4
  137.9 1.0 copy-start
  138.9 1.0 copy-start.2
  139.9 5.9 %collective-permute-start = (f32[512,512]{1,0:T(8,128)S(1)}, f32[512,512]{1,0:T(8,128)}, u32[]{:S(2)}, u32[]{:S(2)}) collective-permute-start(f32[512,512]{1,0:T(8,128)S(1)} %get-tuple-element.11), channel_id=1, source_target_pairs={{0,4},{4,0},{8,12},{12,8},{16,20},{20,16},{24,28},{28,24},{1,5},{5... | collective-permute-start | bytes 3145736 | tf_op jit(solution)/shard_map/ppermute | solution.py:218
  139.9 7.4 %collective-permute-start.9 = (f32[512,512]{1,0:T(8,128)S(1)}, f32[512,512]{1,0:T(8,128)}, u32[]{:S(2)}, u32[]{:S(2)}) collective-permute-start(f32[512,512]{1,0:T(8,128)S(1)} %get-tuple-element.14), channel_id=1, source_target_pairs={{0,4},{4,0},{8,12},{12,8},{16,20},{20,16},{24,28},{28,24},{1,5},{5... | collective-permute-start | bytes 3145736 | tf_op jit(solution)/shard_map/ppermute | solution.py:218
  144.5 1.2 collective-permute-start.3
  146.0 10.8 %collective-permute-start.4 = (f32[256]{0:T(256)S(1)}, f32[256]{0:T(256)S(1)}, u32[]{:S(2)}, u32[]{:S(2)}) collective-permute-start(f32[256]{0:T(256)S(1)} %slice_select_fusion.4), channel_id=1, source_target_pairs={{8,0},{12,4},{24,16},{28,20},{9,1},{13,5},{25,17},{29,21},{10,2},{... | collective-permute-start | bytes 3080 | tf_op jit(solution)/shard_map/ppermute | solution.py:218
  150.7 1.1 copy-start.5
  151.8 15.0 %collective-permute-start.10 = (f32[256,512]{1,0:T(8,128)}, f32[256,512]{1,0:T(8,128)}, u32[]{:S(2)}, u32[]{:S(2)}) collective-permute-start(f32[256,512]{1,0:T(8,128)} %slice_select_fusion.1), channel_id=1, source_target_pairs={{8,0},{12,4},{24,16},{28,20},{9,1},{13,5},{25,17},{29,21},{10,2},{... | collective-permute-start | bytes 1572872 | tf_op jit(solution)/shard_map/ppermute | solution.py:218
  156.7 6.3 %collective-permute-start.5 = (f32[256]{0:T(256)S(1)}, f32[256]{0:T(256)S(1)}, u32[]{:S(2)}, u32[]{:S(2)}) collective-permute-start(f32[256]{0:T(256)S(1)} %collective-permute-done.4), channel_id=1, source_target_pairs={{0,4},{4,0},{8,12},{12,8},{16,20},{20,16},{24,28},{28,24},{1,5},{5... | collective-permute-start | bytes 3080 | tf_op jit(solution)/shard_map/ppermute | solution.py:218
  161.7 17.6 %collective-permute-start.1 = (f32[256,512]{1,0:T(8,128)}, f32[256,512]{1,0:T(8,128)}, u32[]{:S(2)}, u32[]{:S(2)}) collective-permute-start(f32[256,512]{1,0:T(8,128)} %slice_select_fusion.2), channel_id=1, source_target_pairs={{8,0},{12,4},{9,1},{13,5},{10,2},{14,6},{11,3},{15,7}} | collective-permute-start | bytes 1572872 | tf_op jit(solution)/shard_map/ppermute | solution.py:218
  166.8 13.1 %collective-permute-start.11 = (f32[256,512]{1,0:T(8,128)}, f32[256,512]{1,0:T(8,128)}, u32[]{:S(2)}, u32[]{:S(2)}) collective-permute-start(f32[256,512]{1,0:T(8,128)} %collective-permute-done.10), channel_id=1, source_target_pairs={{0,4},{4,0},{8,12},{12,8},{16,20},{20,16},{24,28},{28,24},{1,5},{5... | collective-permute-start | bytes 1572872 | tf_op jit(solution)/shard_map/ppermute | solution.py:218
  171.5 5.5 %collective-permute-start.6 = (f32[256]{0:T(256)S(1)}, f32[256]{0:T(256)S(1)}, u32[]{:S(2)}, u32[]{:S(2)}) collective-permute-start(f32[256]{0:T(256)S(1)} %slice_select_fusion.3), channel_id=1, source_target_pairs={{16,0},{20,4},{17,1},{21,5},{18,2},{22,6},{19,3},{23,7}} | collective-permute-start | bytes 3080 | tf_op jit(solution)/shard_map/ppermute | solution.py:218
  172.8 4.2 %collective-permute-start.7 = (f32[256]{0:T(256)S(1)}, f32[256]{0:T(256)S(1)}, u32[]{:S(2)}, u32[]{:S(2)}) collective-permute-start(f32[256]{0:T(256)S(1)} %slice_select_fusion.3), channel_id=1, source_target_pairs={{16,8},{20,12},{17,9},{21,13},{18,10},{22,14},{19,11},{23,15}} | collective-permute-start | bytes 3080 | tf_op jit(solution)/shard_map/ppermute | solution.py:218
  177.0 1.1 collective-permute-start.8
  179.3 7.5 %collective-permute-start.2 = (f32[256,512]{1,0:T(8,128)}, f32[256,512]{1,0:T(8,128)S(1)}, u32[]{:S(2)}, u32[]{:S(2)}) collective-permute-start(f32[256,512]{1,0:T(8,128)} %collective-permute-done.1), channel_id=1, source_target_pairs={{0,4},{4,0},{8,12},{12,8},{16,20},{20,16},{24,28},{28,24},{1,5},{5... | collective-permute-start | bytes 1572872 | tf_op jit(solution)/shard_map/ppermute | solution.py:218
  184.8 15.7 %collective-permute-start.12 = (f32[256,512]{1,0:T(8,128)S(1)}, f32[256,512]{1,0:T(8,128)S(1)}, u32[]{:S(2)}, u32[]{:S(2)}) collective-permute-start(f32[256,512]{1,0:T(8,128)S(1)} %slice_select_fusion), channel_id=1, source_target_pairs={{16,0},{20,4},{17,1},{21,5},{18,2},{22,6},{19,3},{23,7}} | collective-permute-start | bytes 1572872 | tf_op jit(solution)/shard_map/ppermute | solution.py:218
  186.1 14.4 %collective-permute-start.13 = (f32[256,512]{1,0:T(8,128)S(1)}, f32[256,512]{1,0:T(8,128)S(1)}, u32[]{:S(2)}, u32[]{:S(2)}) collective-permute-start(f32[256,512]{1,0:T(8,128)S(1)} %slice_select_fusion), channel_id=1, source_target_pairs={{16,8},{20,12},{17,9},{21,13},{18,10},{22,14},{19,11},{23,15}} | collective-permute-start | bytes 1572872 | tf_op jit(solution)/shard_map/ppermute | solution.py:218
  200.7 2.9 %collective-permute-start.14 = (f32[256,512]{1,0:T(8,128)S(1)}, f32[256,512]{1,0:T(8,128)S(1)}, u32[]{:S(2)}, u32[]{:S(2)}) collective-permute-start(f32[256,512]{1,0:T(8,128)S(1)} %add.96), channel_id=1, source_target_pairs={{0,4},{4,0},{8,12},{12,8},{16,20},{20,16},{24,28},{28,24},{1,5},{5... | collective-permute-start | bytes 1572872 | tf_op jit(solution)/shard_map/ppermute | solution.py:218
  204.6 3.6 %copy-start.1 = (f32[4,128,512]{2,1,0:T(8,128)S(1)}, f32[4,128,512]{2,1,0:T(8,128)}, u32[]{:S(2)}) copy-start(f32[4,128,512]{2,1,0:T(8,128)} %copy-done) | copy-start | bytes 3145732
  205.7 5.1 %copy-start.6 = (f32[512,512]{1,0:T(8,128)S(1)}, f32[512,512]{1,0:T(8,128)}, u32[]{:S(2)}) copy-start(f32[512,512]{1,0:T(8,128)} %get-tuple-element.17) | copy-start | bytes 3145732
  205.7 5.8 %copy-start.3 = (f32[512,512]{1,0:T(8,128)S(1)}, f32[512,512]{1,0:T(8,128)}, u32[]{:S(2)}) copy-start(f32[512,512]{1,0:T(8,128)} %copy-done.2) | copy-start | bytes 3145732

commit v4 on v3

--- a/solution.py
+++ b/solution.py
@@ -40,14 +40,8 @@
 
 
 def send_order(steps, hops):
-    order, reached, at = [], [0] * steps, [-2] * steps
-    while len(order) < steps * hops:
-        ready = [k for k in range(steps) if reached[k] < hops]
-        k = next((k for k in ready if at[k] <= len(order) - 2), ready[0])
-        order.append((k, reached[k]))
-        reached[k] += 1
-        at[k] = len(order) - 1
-    return order
+    sends = [(k, hop) for hop in range(hops) for k in range(steps)]
+    return sorted(sends, key=lambda send: 3 * send[1] + send[0] + send[0] // 3)
 
 
 def block_kernel(
@@ -103,7 +97,7 @@
             pump(1)
         land(k, n - 2)
 
-    pump(2)
+    pump(3)
     for d, peer in enumerate(peers):
         small = copy(g_ref, offsets_ref.at[me], g_send.at[d], g_recv.at[d], peer)
         small.start()
@@ -123,7 +117,7 @@
 
     for k in range(steps - 2, -1, -1):
         complete(k)
-        pump(2)
+        pump(3)
         columns_ref[k] = three_pass(whole_ref[k], covs_ref[k + 1], 1)
         swaps = []
         for d, peer in enumerate(peers):
@@ -136,8 +130,7 @@
         pieces_ref[k, me] = columns_ref[k, part(me)]
         if k == steps - 2:
             complete(steps - 1)
-            pump(1)
-        if k > 0:
+            pump(len(order))
             compose(k)
         for swap in swaps:
             swap.wait_recv()
@@ -146,6 +139,7 @@
         covs_ref[k] = three_pass(pieces, whole_ref[k], 1) + l_ref[k]
 
     kept = n // 2 + 1
+    later = list(range(steps - 3, -1, -1))
     for j in range(kept):
         at = part(lax.rem(me + j, n))
         cov_ref[part(me), at] = covs_ref[0, :, at]
@@ -160,11 +154,13 @@
             )
             move.start()
             moves.append(move)
-        if hop == 0:
-            compose(0)
+        if later:
+            compose(later.pop(0))
         for move in moves:
             move.wait_recv()
         sent.extend(moves)
+    for k in later:
+        compose(k)
     for p in range(n):
         for j in range(kept, n):
             q = (p + j) % n

time: 214 us -> 199 us (0.930)
  Pallas kernels: 137 us -> 122 us
    pallas_call x1, Pallas kernels: 137 us -> 122 us  [block_element(): pl.pallas_call(functools.partial(block_kernel, n), out_shape=(jax.ShapeDt...]
  transfers between devices with their start and end apart: 15 -> 15, of which waited for: 6 -> 6; matrix products, arithmetic and copies ran while one was open for 14% -> 15% of each run, Pallas kernels for 0% -> 0%
where the time goes in v4:
time: 199 us; the launch traced here: 198 us
  Pallas kernels  122 us (61%)
  matrix products  27.2 us (14%)
  waiting for transfers between devices  17.8 us (9%)
  starting transfers between devices  15 us (8%)
  other arithmetic  11.2 us (6%)
  local copies, waits for them, and re-layouts  4.47 us (2%)
    pallas_call x1, Pallas kernels, block_element(): pl.pallas_call(functools.partial(block_kernel, n), out_shape=(jax.ShapeDt...  122 us
    ppermute x15, waiting for transfers between devices, send(): return lax.ppermute(value, 'tm', pairs)  17.8 us
    dot_general x7, matrix products, product(): jnp.dot(left, right, precision=lax.Precision.HIGH, preferred_element_type...  16.6 us
    ppermute x15, starting transfers between devices, send(): return lax.ppermute(value, 'tm', pairs)  15 us
    dot_general x8, matrix products, product_t(): lax.dot_general(left, right, (((1,), (1,)), ((), ())), precision=lax.Prec...  10.6 us
    reduce_sum x6, other arithmetic, matvec(): return jnp.sum(matrix * vector[None, :], axis=1)  6.28 us
  transfers between devices with their start and end apart: 15, of which 6 were waited for; matrix products, arithmetic and copies ran while one was open for 15% of the time, Pallas kernels for 0%

profile of v4, /device:TPU:0, one launch (start us, length us, event | category | flops | bytes accessed | tf_op | source)
XLA Modules:
  0.0 198.3 jit_solution(3241415327069758179)
XLA Ops:
  0.6 0.7 copy-done.4
  1.3 121.6 %shard_map.50 = (f32[4,512,512]{2,1,0:T(8,128)}, f32[4,128,512]{2,1,0:T(8,128)S(1)}, f32[4,128,512]{2,1,0:T(8,128)S(1)}, f32[512,512]{1,0:T(8,128)S(1)}, f32[4,4...) custom-call(f32[4,128,512]{2,1,0:T(8,128)} %e_ref.1, ...), custom_call_target="tpu_custom_call" | custom-call | flops 2415919104 | bytes 12582912 | tf_op jit(solution)/shard_map/pallas_call | solution.py:185
  122.9 1.0 copy-done
  123.9 1.0 copy-done.2
  124.9 0.0 collective-permute-start
  124.9 0.5 collective-permute-start.9
  125.4 1.4 fusion.17
  126.8 1.4 fusion.18
  128.2 1.4 fusion.19
  129.6 0.1 collective-permute-start.3
  129.7 1.1 collective-permute-done.3
  130.8 0.0 collective-permute-done
  130.8 0.2 multiply_reduce_fusion.4
  131.0 1.3 collective-permute-start.4
  132.3 2.3 %fusion.22 = f32[512,512]{1,0:T(8,128)S(1)} fusion(f32[512,512]{1,0:T(8,128)} %collective-permute-done.9, f32[512,512]{1,0:T(8,128)S(1)} %get-tuple-element.14, pred[]{:T(512)S(6)} %eq.14, f32[512,512]{1,0:T(8,128)S(1)} %get-tuple-element.11, f32[512,512]{1,0:T(8,128)} %collective-permute-done), kind=kOutput, calls=%fused_computation.38 | convolution fusion | flops 805830656 | bytes 5242881 | tf_op jit(solution)/shard_map/dot_general | solution.py:12
  134.6 1.1 convolution_add_fusion.1
  135.8 1.0 slice_select_fusion.1
  136.7 0.2 copy-done.5
  136.9 1.3 collective-permute-start.10
  138.2 2.3 %fusion.24 = f32[512,512]{0,1:T(8,128)S(1)} fusion(f32[512,512]{1,0:T(8,128)} %collective-permute-done, f32[512,512]{1,0:T(8,128)S(1)} %get-tuple-element.11, pred[]{:T(512)S(6)} %eq.14), kind=kOutput, calls=%fused_computation.45 | convolution fusion | flops 805830656 | bytes 3145729 | tf_op jit(solution)/shard_map/dot_general | solution.py:12
  140.5 1.3 copy.5
  141.8 0.0 collective-permute-done.4
  141.8 2.9 %collective-permute-start.5 = (f32[256]{0:T(256)S(1)}, f32[256]{0:T(256)S(1)}, u32[]{:S(2)}, u32[]{:S(2)}) collective-permute-start(f32[256]{0:T(256)S(1)} %collective-permute-done.4), channel_id=1, source_target_pairs={{0,4},{4,0},{8,12},{12,8},{16,20},{20,16},{24,28},{28,24},{1,5},{5... | collective-permute-start | bytes 3080 | tf_op jit(solution)/shard_map/ppermute | solution.py:214
  144.7 2.1 %slice_select_fusion.2 = f32[256,512]{1,0:T(8,128)} fusion(f32[512,512]{1,0:T(8,128)} %copy.5, pred[]{:T(512)S(6)} %eq.14), kind=kLoop, calls=%fused_computation.54 | loop fusion | flops 131072 | bytes 1572865 | tf_op jit(solution)/shard_map/jit(_where)/select_n | solution.py:219
  146.8 1.3 collective-permute-start.1
  148.1 0.0 collective-permute-done.5
  148.1 3.7 %collective-permute-done.10 = f32[256,512]{1,0:T(8,128)} collective-permute-done((f32[256,512]{1,0:T(8,128)}, f32[256,512]{1,0:T(8,128)}, u32[]{:S(2)}, u32[]{:S(2)}) %collective-permute-start.10) | collective-permute-done | bytes 524320 | tf_op jit(solution)/shard_map/ppermute | solution.py:214
  151.9 2.9 %collective-permute-start.11 = (f32[256,512]{1,0:T(8,128)}, f32[256,512]{1,0:T(8,128)}, u32[]{:S(2)}, u32[]{:S(2)}) collective-permute-start(f32[256,512]{1,0:T(8,128)} %collective-permute-done.10), channel_id=1, source_target_pairs={{0,4},{4,0},{8,12},{12,8},{16,20},{20,16},{24,28},{28,24},{1,5},{5... | collective-permute-start | bytes 1572872 | tf_op jit(solution)/shard_map/ppermute | solution.py:214
  154.7 1.8 multiply_reduce_fusion.1
  156.6 1.3 collective-permute-start.6
  157.9 0.8 collective-permute-start.7
  158.7 3.3 %collective-permute-done.6 = f32[256]{0:T(256)S(1)} collective-permute-done((f32[256]{0:T(256)S(1)}, f32[256]{0:T(256)S(1)}, u32[]{:S(2)}, u32[]{:S(2)}) %collective-permute-start.6) | collective-permute-done | bytes 1056 | tf_op jit(solution)/shard_map/ppermute | solution.py:214
  162.0 0.0 collective-permute-done.7
  162.0 0.0 collective-permute-start.8
  162.0 0.1 dynamic_slice.15
  162.1 0.1 dynamic_slice.14
  162.2 0.1 dynamic_slice.13
  162.3 0.1 dynamic_slice.12
  162.3 0.8 collective-permute-done.8
  163.2 1.2 collective-permute-done.1
  164.4 0.5 collective-permute-start.2
  164.9 0.0 collective-permute-done.11
  164.9 2.6 %fusion.28 = f32[512,512]{1,0:T(8,128)S(1)} fusion(f32[512,512]{0,1:T(8,128)S(1)} %fusion.24, f32[256,512]{1,0:T(8,128)} %collective-permute-done.11, f32[256,512]{1,0:T(8,128)} %collective-permute-done.10, pred[]{:T(512)S(6)} %eq.14), kind=kOutput, calls=%fused_computation.51 | convolution fusion | flops 806092800 | bytes 3145729 | tf_op jit(solution)/shard_map/dot_general | solution.py:12
  167.6 2.2 %convolution_add_fusion = f32[512,512]{1,0:T(8,128)S(1)} fusion(f32[512,512]{1,0:T(8,128)} %copy-done.5, f32[512,512]{1,0:T(8,128)S(1)} %fusion.28, f32[512,512]{0,1:T(8,128)S(1)} %fusion.24), kind=kOutput, calls=%fused_computation.3 | convolution fusion | flops 805568512 | bytes 4194304 | tf_op jit(solution)/shard_map/dot_general | solution.py:16
  169.8 0.1 slice_select_fusion
  169.9 1.3 collective-permute-start.12
  171.2 0.7 collective-permute-start.13
  171.9 0.0 collective-permute-done.2
  171.9 3.0 %multiply_reduce_fusion.2 = (f32[512]{0:T(512)S(1)}, f32[512,512]{1,0:T(8,128)S(1)}) fusion(f32[512]{0:T(512)S(1)} %maximum_select_fusion.8, f32[512,512]{1,0:T(8,128)} %collective-permute-done, pred[]{:T(512)S(6)} %eq.14, f32[256,512]{1,0:T(8,128)S(1)} %collective-permute-done.2, f32[256,512]{1,0:T(8,128)} %collective-permute-done.1, pred[]{:T(512)S(6)} %eq.13), kind=kOutput, calls=%fused_computation.42 | convolution fusion | flops 808451584 | bytes 3149826 | tf_op jit(solution)/shard_map/dot_general | solution.py:12
  175.0 0.2 multiply_reduce_fusion
  175.1 2.9 %fusion.26 = f32[512,512]{1,0:T(8,128)S(1)} fusion(f32[512,512]{1,0:T(8,128)} %collective-permute-done, f32[256,512]{1,0:T(8,128)} %collective-permute-done.11, f32[256,512]{1,0:T(8,128)} %collective-permute-done.10, pred[]{:T(512)S(6)} %eq.14), kind=kOutput, calls=%fused_computation.49 | convolution fusion | flops 806879232 | bytes 3145729 | tf_op jit(solution)/shard_map/dot_general | solution.py:12
  178.0 7.6 %collective-permute-done.12 = f32[256,512]{1,0:T(8,128)S(1)} collective-permute-done((f32[256,512]{1,0:T(8,128)S(1)}, f32[256,512]{1,0:T(8,128)S(1)}, u32[]{:S(2)}, u32[]{:S(2)}) %collective-permute-start.12) | collective-permute-done | bytes 524320 | tf_op jit(solution)/shard_map/ppermute | solution.py:214
  185.6 0.1 add.96
  185.7 0.1 collective-permute-start.14
  185.8 0.6 fusion.44
  186.4 2.3 %fusion.27 = f32[512,512]{1,0:T(8,128)S(1)} fusion(f32[512,512]{1,0:T(8,128)S(1)} %fusion.26, f32[512,512]{1,0:T(8,128)} %collective-permute-done, pred[]{:T(512)S(6)} %eq.14), kind=kOutput, calls=%fused_computation.50 | convolution fusion | flops 806092800 | bytes 3145729 | tf_op jit(solution)/shard_map/dot_general | solution.py:16
  188.7 1.0 fusion.10
  189.7 1.1 fusion.51
  190.8 2.5 %fusion.4 = f32[512,512]{1,0:T(8,128)S(1)} fusion(f32[512,512]{1,0:T(8,128)S(1)} %bitcast.53, f32[512,512]{1,0:T(8,128)S(1)} %fusion.51, f32[512,512]{1,0:T(8,128)S(1)} %fusion.27, f32[512,512]{1,0:T(8,128)} %collective-permute-done.9, pred[]{:T(512)S(6)} %eq.12, pred[]{:T(512)S(6)} %eq.14, pred[]{:T(512)S(6)} %eq.13), kind=kOutput, calls=%fused_computation.13 | convolution fusion | flops 806617088 | bytes 5242883 | tf_op jit(solution)/shard_map/dot_general | solution.py:12
  193.3 1.9 fusion
  195.2 0.7 fusion.3
  195.9 0.7 fusion.1
  196.6 0.7 fusion.2
  197.3 1.0 pad_maximum_fusion
  (26 shorter events, 0.1 us)
Async XLA Ops:
  0.6 0.7 copy-start.4
  122.9 1.0 copy-start
  123.9 1.0 copy-start.2
  124.9 5.9 %collective-permute-start = (f32[512,512]{1,0:T(8,128)S(1)}, f32[512,512]{1,0:T(8,128)}, u32[]{:S(2)}, u32[]{:S(2)}) collective-permute-start(f32[512,512]{1,0:T(8,128)S(1)} %get-tuple-element.11), channel_id=1, source_target_pairs={{0,4},{4,0},{8,12},{12,8},{16,20},{20,16},{24,28},{28,24},{1,5},{5... | collective-permute-start | bytes 3145736 | tf_op jit(solution)/shard_map/ppermute | solution.py:214
  124.9 7.4 %collective-permute-start.9 = (f32[512,512]{1,0:T(8,128)S(1)}, f32[512,512]{1,0:T(8,128)}, u32[]{:S(2)}, u32[]{:S(2)}) collective-permute-start(f32[512,512]{1,0:T(8,128)S(1)} %get-tuple-element.14), channel_id=1, source_target_pairs={{0,4},{4,0},{8,12},{12,8},{16,20},{20,16},{24,28},{28,24},{1,5},{5... | collective-permute-start | bytes 3145736 | tf_op jit(solution)/shard_map/ppermute | solution.py:214
  129.6 1.2 collective-permute-start.3
  131.0 10.8 %collective-permute-start.4 = (f32[256]{0:T(256)S(1)}, f32[256]{0:T(256)S(1)}, u32[]{:S(2)}, u32[]{:S(2)}) collective-permute-start(f32[256]{0:T(256)S(1)} %slice_select_fusion.4), channel_id=1, source_target_pairs={{8,0},{12,4},{24,16},{28,20},{9,1},{13,5},{25,17},{29,21},{10,2},{... | collective-permute-start | bytes 3080 | tf_op jit(solution)/shard_map/ppermute | solution.py:214
  135.7 1.1 copy-start.5
  136.9 15.0 %collective-permute-start.10 = (f32[256,512]{1,0:T(8,128)}, f32[256,512]{1,0:T(8,128)}, u32[]{:S(2)}, u32[]{:S(2)}) collective-permute-start(f32[256,512]{1,0:T(8,128)} %slice_select_fusion.1), channel_id=1, source_target_pairs={{8,0},{12,4},{24,16},{28,20},{9,1},{13,5},{25,17},{29,21},{10,2},{... | collective-permute-start | bytes 1572872 | tf_op jit(solution)/shard_map/ppermute | solution.py:214
  141.8 6.3 %collective-permute-start.5 = (f32[256]{0:T(256)S(1)}, f32[256]{0:T(256)S(1)}, u32[]{:S(2)}, u32[]{:S(2)}) collective-permute-start(f32[256]{0:T(256)S(1)} %collective-permute-done.4), channel_id=1, source_target_pairs={{0,4},{4,0},{8,12},{12,8},{16,20},{20,16},{24,28},{28,24},{1,5},{5... | collective-permute-start | bytes 3080 | tf_op jit(solution)/shard_map/ppermute | solution.py:214
  146.8 17.6 %collective-permute-start.1 = (f32[256,512]{1,0:T(8,128)}, f32[256,512]{1,0:T(8,128)}, u32[]{:S(2)}, u32[]{:S(2)}) collective-permute-start(f32[256,512]{1,0:T(8,128)} %slice_select_fusion.2), channel_id=1, source_target_pairs={{8,0},{12,4},{9,1},{13,5},{10,2},{14,6},{11,3},{15,7}} | collective-permute-start | bytes 1572872 | tf_op jit(solution)/shard_map/ppermute | solution.py:214
  151.9 13.1 %collective-permute-start.11 = (f32[256,512]{1,0:T(8,128)}, f32[256,512]{1,0:T(8,128)}, u32[]{:S(2)}, u32[]{:S(2)}) collective-permute-start(f32[256,512]{1,0:T(8,128)} %collective-permute-done.10), channel_id=1, source_target_pairs={{0,4},{4,0},{8,12},{12,8},{16,20},{20,16},{24,28},{28,24},{1,5},{5... | collective-permute-start | bytes 1572872 | tf_op jit(solution)/shard_map/ppermute | solution.py:214
  156.6 5.5 %collective-permute-start.6 = (f32[256]{0:T(256)S(1)}, f32[256]{0:T(256)S(1)}, u32[]{:S(2)}, u32[]{:S(2)}) collective-permute-start(f32[256]{0:T(256)S(1)} %slice_select_fusion.3), channel_id=1, source_target_pairs={{16,0},{20,4},{17,1},{21,5},{18,2},{22,6},{19,3},{23,7}} | collective-permute-start | bytes 3080 | tf_op jit(solution)/shard_map/ppermute | solution.py:214
  157.9 4.2 %collective-permute-start.7 = (f32[256]{0:T(256)S(1)}, f32[256]{0:T(256)S(1)}, u32[]{:S(2)}, u32[]{:S(2)}) collective-permute-start(f32[256]{0:T(256)S(1)} %slice_select_fusion.3), channel_id=1, source_target_pairs={{16,8},{20,12},{17,9},{21,13},{18,10},{22,14},{19,11},{23,15}} | collective-permute-start | bytes 3080 | tf_op jit(solution)/shard_map/ppermute | solution.py:214
  162.0 1.1 collective-permute-start.8
  164.4 7.5 %collective-permute-start.2 = (f32[256,512]{1,0:T(8,128)}, f32[256,512]{1,0:T(8,128)S(1)}, u32[]{:S(2)}, u32[]{:S(2)}) collective-permute-start(f32[256,512]{1,0:T(8,128)} %collective-permute-done.1), channel_id=1, source_target_pairs={{0,4},{4,0},{8,12},{12,8},{16,20},{20,16},{24,28},{28,24},{1,5},{5... | collective-permute-start | bytes 1572872 | tf_op jit(solution)/shard_map/ppermute | solution.py:214
  169.9 15.7 %collective-permute-start.12 = (f32[256,512]{1,0:T(8,128)S(1)}, f32[256,512]{1,0:T(8,128)S(1)}, u32[]{:S(2)}, u32[]{:S(2)}) collective-permute-start(f32[256,512]{1,0:T(8,128)S(1)} %slice_select_fusion), channel_id=1, source_target_pairs={{16,0},{20,4},{17,1},{21,5},{18,2},{22,6},{19,3},{23,7}} | collective-permute-start | bytes 1572872 | tf_op jit(solution)/shard_map/ppermute | solution.py:214
  171.2 14.4 %collective-permute-start.13 = (f32[256,512]{1,0:T(8,128)S(1)}, f32[256,512]{1,0:T(8,128)S(1)}, u32[]{:S(2)}, u32[]{:S(2)}) collective-permute-start(f32[256,512]{1,0:T(8,128)S(1)} %slice_select_fusion), channel_id=1, source_target_pairs={{16,8},{20,12},{17,9},{21,13},{18,10},{22,14},{19,11},{23,15}} | collective-permute-start | bytes 1572872 | tf_op jit(solution)/shard_map/ppermute | solution.py:214
  185.7 2.9 %collective-permute-start.14 = (f32[256,512]{1,0:T(8,128)S(1)}, f32[256,512]{1,0:T(8,128)S(1)}, u32[]{:S(2)}, u32[]{:S(2)}) collective-permute-start(f32[256,512]{1,0:T(8,128)S(1)} %add.96), channel_id=1, source_target_pairs={{0,4},{4,0},{8,12},{12,8},{16,20},{20,16},{24,28},{28,24},{1,5},{5... | collective-permute-start | bytes 1572872 | tf_op jit(solution)/shard_map/ppermute | solution.py:214
  189.7 3.6 %copy-start.1 = (f32[4,128,512]{2,1,0:T(8,128)S(1)}, f32[4,128,512]{2,1,0:T(8,128)}, u32[]{:S(2)}) copy-start(f32[4,128,512]{2,1,0:T(8,128)} %copy-done) | copy-start | bytes 3145732
  190.8 5.1 %copy-start.6 = (f32[512,512]{1,0:T(8,128)S(1)}, f32[512,512]{1,0:T(8,128)}, u32[]{:S(2)}) copy-start(f32[512,512]{1,0:T(8,128)} %get-tuple-element.17) | copy-start | bytes 3145732
  190.8 5.8 %copy-start.3 = (f32[512,512]{1,0:T(8,128)S(1)}, f32[512,512]{1,0:T(8,128)}, u32[]{:S(2)}) copy-start(f32[512,512]{1,0:T(8,128)} %copy-done.2) | copy-start | bytes 3145732

commit v5 on v4

--- a/solution.py
+++ b/solution.py
@@ -45,7 +45,7 @@
 
 
 def block_kernel(
-    n, e_ref, g_ref, l_ref, whole_ref, own_ref, covs_ref, cov_ref, offsets_ref, *more
+    n, e_ref, g_ref, l_ref, whole_ref, own_ref, covs_ref, cov_ref, offsets_ref, means_ref, *more
 ):
     steps, rows, width = e_ref.shape
     gains = more[: steps - 1]
@@ -161,6 +161,16 @@
         sent.extend(moves)
     for k in later:
         compose(k)
+    for small in smalls:
+        small.wait_recv()
+    for k in range(steps - 1, -1, -1):
+        row = jnp.concatenate([offsets_ref[p, k : k + 1] for p in range(n)], axis=1)
+        row = jnp.broadcast_to(row, (8, width))
+        if k < steps - 1:
+            row = three_pass(means_ref[k + 1], whole_ref[k], 1) + row
+        means_ref[k] = row
+    cov_ref[width : width + 8] = means_ref[0]
+    cov_ref[width + 8 :] = jnp.zeros((8, width), jnp.float32)
     for p in range(n):
         for j in range(kept, n):
             q = (p + j) % n
@@ -170,8 +180,6 @@
     own_ref[steps - 1] = e_ref[steps - 1]
     for k in range(steps - 1):
         own_ref[k] = gains[k][part(me)]
-    for small in smalls:
-        small.wait_recv()
     for move in [*ring.values(), *sent]:
         move.wait_send()
 
@@ -188,12 +196,13 @@
             jax.ShapeDtypeStruct((steps, width, width), f32),
             jax.ShapeDtypeStruct((steps, rows, width), f32),
             jax.ShapeDtypeStruct((steps, rows, width), f32),
-            jax.ShapeDtypeStruct((width, width), f32),
+            jax.ShapeDtypeStruct((width + 16, width), f32),
             jax.ShapeDtypeStruct((n, steps, rows), f32),
+            jax.ShapeDtypeStruct((steps, 8, width), f32),
             *[jax.ShapeDtypeStruct((width, width), f32)] * (steps - 1),
         ),
         in_specs=[vmem] * 3,
-        out_specs=(vmem,) * (steps + 4),
+        out_specs=(vmem,) * (steps + 5),
         scratch_shapes=[
             pltpu.VMEM((steps - 1, width, rows), f32),
             pltpu.VMEM((steps - 1, n, rows, rows), f32),
@@ -208,6 +217,227 @@
             flops=18 * width**3, bytes_accessed=12 * 2**20, transcendentals=0
         ),
     )(transitions, offsets, noise_cov)
+
+
+def scan_kernel(blocks, cov_ref, own_ref, covs_ref, *more):
+    steps, rows, width = covs_ref.shape
+    gains = more[:steps]
+    (out_ref, mean_ref, swap_a, swap_c, first, later_c, g_a, g_c, x_a, x_c, got_a, got_c,
+     s_send, s_recv, c_send, c_recv, cw_send, cw_recv, a_send, a_recv, aw_send,
+     aw_recv) = more[steps:]
+    a_ref = gains[0]
+    f32 = jnp.float32
+    me = lax.axis_index("tm")
+    core = lax.rem(me, 2)
+    partner = me + 1 - 2 * core
+    tile_rows = 256
+
+    def copy(source, target, send_sem, recv_sem, peer):
+        return pltpu.make_async_remote_copy(
+            src_ref=source, dst_ref=target, send_sem=send_sem, recv_sem=recv_sem,
+            device_id={"tm": peer}, device_id_type=pl.DeviceIdType.MESH,
+        )
+
+    def tiles(body):
+        @pl.loop(0, width // tile_rows)
+        def _(tile):
+            body(pl.ds(pl.multiple_of(tile * tile_rows, tile_rows), tile_rows))
+
+    def join(out, gain, cov, add):
+        def body(at):
+            left = three_pass(gain[at], cov[:width], 0)
+            out[at] = three_pass(left, gain[...], 1) + add(at)
+
+        tiles(body)
+        tail = pl.ds(width, 8)
+        out[tail] = three_pass(cov[tail], gain[...], 1) + add(tail)
+
+    def times(out, left, right):
+        def body(at):
+            out[at] = three_pass(left[at], right(), 0)
+
+        tiles(body)
+
+    levels = []
+    distance = 2
+    while distance < blocks:
+        levels.append(distance)
+        distance *= 2
+
+    def half(ref):
+        size = ref.shape[0] // 2
+        return ref.at[pl.ds(pl.multiple_of(core * size, 8), size)]
+
+    def place(level):
+        return lax.rem(me, 2 * levels[level])
+
+    def holds(level):
+        at = place(level)
+        return (at >= levels[level]) & (at < levels[level] + 2)
+
+    def lower(level):
+        return place(level) < levels[level]
+
+    def inner(level):
+        return me < blocks - 2 * levels[level]
+
+    def sends(level, source, target, send_sem, recv_sem):
+        d = levels[level]
+        return [
+            copy(half(source), half(target.at[level]), send_sem.at[level, q],
+                 recv_sem.at[level], me - d + 2 * q)
+            for q in range(d // 2)
+        ]
+
+    def c_sends(level):
+        return sends(level, g_c, got_c, c_send, c_recv)
+
+    def a_sends(level):
+        return sends(level, g_a, got_a, a_send, a_recv)
+
+    def relay(level, target, send_sem, recv_sem):
+        part = half(target.at[level])
+        return copy(part, part, send_sem.at[level], recv_sem.at[level], partner)
+
+    def receive(level, target, recv_sem, w_send, w_recv):
+        part = half(target.at[level])
+        copy(part, part, w_send.at[level], recv_sem.at[level], partner).wait_recv()
+        move = relay(level, target, w_send, w_recv)
+        move.start()
+        move.wait_recv()
+
+    def start_c(level):
+        @pl.when(holds(level))
+        def _():
+            for move in c_sends(level):
+                move.start()
+
+    def start_a(level):
+        if level < len(levels) - 1:
+            @pl.when(holds(level) & inner(level))
+            def _():
+                for move in a_sends(level):
+                    move.start()
+
+    barrier = pltpu.get_barrier_semaphore()
+    for d in range(1, blocks):
+        pl.semaphore_signal(
+            barrier, inc=1, device_id={"tm": lax.rem(me + d, blocks)},
+            device_id_type=pl.DeviceIdType.MESH,
+        )
+    pl.semaphore_wait(barrier, blocks - 1)
+
+    swaps = [
+        copy(cov_ref, swap_c, s_send.at[0], s_recv.at[0], partner),
+        copy(a_ref, swap_a, s_send.at[1], s_recv.at[1], partner),
+    ]
+    for move in swaps:
+        move.start()
+    for move in swaps:
+        move.wait_recv()
+    early = core == 0
+    first[...] = jnp.where(early, a_ref[...], swap_a[...])
+    later_c[...] = jnp.where(early, swap_c[...], cov_ref[...])
+    g_c[width:] = jnp.zeros((16, width), f32)
+    join(g_c, first, later_c, lambda at: jnp.where(early, cov_ref[at], swap_c[at]))
+    start_c(0)
+    times(g_a, first, lambda: jnp.where(early, swap_a[...], a_ref[...]))
+    start_a(0)
+    row = lax.broadcasted_iota(jnp.int32, (width, width), 0)
+    column = lax.broadcasted_iota(jnp.int32, (width, width), 1)
+    x_a[...] = jnp.where(early, swap_a[...], (row == column).astype(f32))
+    x_c[...] = jnp.where(early, swap_c[...], 0.0)
+
+    for level in range(len(levels)):
+        final = level == len(levels) - 1
+
+        @pl.when(lower(level))
+        def _():
+            receive(level, got_c, c_recv, cw_send, cw_recv)
+
+        if not final:
+            @pl.when(place(level) < 2)
+            def _():
+                join(g_c, g_a, got_c.at[level], lambda at: g_c[at])
+
+            start_c(level + 1)
+
+        @pl.when(lower(level))
+        def _():
+            join(x_c, x_a, got_c.at[level], lambda at: x_c[at])
+
+        if not final:
+            @pl.when(lower(level) & inner(level))
+            def _():
+                receive(level, got_a, a_recv, aw_send, aw_recv)
+                times(x_a, x_a, lambda: got_a[level])
+
+            @pl.when((place(level) < 2) & inner(level))
+            def _():
+                times(g_a, g_a, lambda: got_a[level])
+
+            start_a(level + 1)
+
+    for k in range(steps):
+        left = three_pass(own_ref[k * rows : (k + 1) * rows], x_c[:width], 0)
+        out_ref[k] = three_pass(left, gains[k][...], 1) + covs_ref[k]
+    mean_ref[...] = three_pass(x_c[width : width + 8], own_ref[...], 1)
+
+    for move in swaps:
+        move.wait_send()
+    for level in range(len(levels)):
+        @pl.when(holds(level))
+        def _():
+            for move in c_sends(level):
+                move.wait_send()
+
+        @pl.when(lower(level))
+        def _():
+            relay(level, got_c, cw_send, cw_recv).wait_send()
+
+        if level < len(levels) - 1:
+            @pl.when(holds(level) & inner(level))
+            def _():
+                for move in a_sends(level):
+                    move.wait_send()
+
+            @pl.when(lower(level) & inner(level))
+            def _():
+                relay(level, got_a, aw_send, aw_recv).wait_send()
+
+
+def scan_and_smooth(cov, own, covs, gains):
+    steps, rows, width = covs.shape
+    blocks = lax.axis_size("tm")
+    f32 = jnp.float32
+    vmem = pl.BlockSpec(memory_space=pltpu.VMEM)
+    dma = pltpu.SemaphoreType.DMA
+    levels = blocks.bit_length() - 2
+    square, tall = pltpu.VMEM((width, width), f32), pltpu.VMEM((width + 16, width), f32)
+    out, mean = pl.pallas_call(
+        functools.partial(scan_kernel, blocks),
+        out_shape=(
+            jax.ShapeDtypeStruct((steps, rows, width), f32),
+            jax.ShapeDtypeStruct((8, steps * rows), f32),
+        ),
+        in_specs=[vmem] * (3 + steps),
+        out_specs=(vmem, vmem),
+        scratch_shapes=[
+            square, tall, square, tall, square, tall, square, tall,
+            pltpu.VMEM((levels, width, width), f32),
+            pltpu.VMEM((levels, width + 16, width), f32),
+            dma((2,)), dma((2,)), dma((levels, blocks // 4)), dma((levels,)),
+            dma((levels,)), dma((levels,)), dma((levels, blocks // 4)), dma((levels,)),
+            dma((levels,)), dma((levels,)),
+        ],
+        compiler_params=pltpu.CompilerParams(
+            collective_id=1, has_side_effects=True, vmem_limit_bytes=48 * 2**20
+        ),
+        cost_estimate=pl.CostEstimate(
+            flops=24 * width**3, bytes_accessed=12 * 2**20, transcendentals=0
+        ),
+    )(cov, own, covs, *gains)
+    return mean, out
 
 
 def send(value, pairs):
@@ -273,18 +503,14 @@
 def per_device(transitions, offsets, noise_cov):
     steps, rows = transitions.shape[:2]
     start = lax.axis_index("panel") * rows
-    if rows % 128 == 0 and steps > 1:
-        whole, own, covs, whole_cov, parts, *composed = block_element(
+    if rows % 128 == 0 and steps > 1 and lax.axis_size("tm") > 2:
+        whole, own, covs, whole_cov, _, means, *composed = block_element(
             transitions, offsets, noise_cov
         )
-        all_offsets = jnp.swapaxes(parts, 0, 1).reshape(steps, -1)
-        gains = [whole[steps - 1], *(composed[k] for k in range(steps - 2, -1, -1))]
-        means = [all_offsets[steps - 1]]
-        for k in range(steps - 2, -1, -1):
-            means.append(matvec(whole[k], means[-1]) + all_offsets[k])
-        covs = [covs[k] for k in range(steps - 1, -1, -1)]
-        gain, offset = gains[-1], means[-1]
-        own = own.reshape(steps * rows, -1)
+        gains = [*composed, whole[steps - 1]]
+        mean, out = scan_and_smooth(whole_cov, own.reshape(steps * rows, -1), covs, gains)
+        rows_mean = lax.dynamic_slice_in_dim(means[:, 0], start, rows, 1)
+        return mean[0].reshape(steps, rows) + rows_mean, out
     else:
         whole = {}
         for k in [*range(steps - 2, -1, -1), steps - 1]:

time: 199 us -> 180 us (0.905)
  Pallas kernels: 122 us -> 173 us
  matrix products: 27.2 us -> 0 us
  waiting for transfers between devices: 17.8 us -> 0 us
  starting transfers between devices: 15 us -> 0 us
  other arithmetic: 11.2 us -> 0.58 us
    pallas_call x0 -> x1, Pallas kernels: none -> 50.3 us  [scan_and_smooth(): pl.pallas_call(functools.partial(scan_kernel, blocks), out_shape=(jax.Sha...]
    dot_general x15 -> x0, matrix products: 27.2 us -> none  [the longest x7 16.6 us: product(): jnp.dot(left, right, precision=lax.Precision.HIGH, preferred_element_type...]
    ppermute x15 -> x0, waiting for transfers between devices: 17.8 us -> none  [send(): return lax.ppermute(value, 'tm', pairs)]
    ppermute x15 -> x0, starting transfers between devices: 15 us -> none  [send(): return lax.ppermute(value, 'tm', pairs)]
    reduce_sum x6 -> x0, other arithmetic: 6.28 us -> none  [matvec(): return jnp.sum(matrix * vector[None, :], axis=1)]
    select_n x9 -> x0, other arithmetic: 3.15 us -> none  [the longest x5 3.12 us: spread(): own = jnp.where(core == 0, value[:half], value[half:])]
    squeeze x0 -> x1, local copies, waits for them, and re-layouts: none -> 2.3 us  [per_device(): gains = [*composed, whole[steps - 1]]]
  transfers between devices with their start and end apart: 15 -> 0, of which waited for: 6 -> 0; matrix products, arithmetic and copies ran while one was open for 15% -> 0% of each run, Pallas kernels for 0% -> 0%
where the time goes in v5:
time: 180 us; the launch traced here: 179 us
  Pallas kernels  173 us (96%)
  local copies, waits for them, and re-layouts  4.92 us (3%)
    pallas_call x1, Pallas kernels, block_element(): pl.pallas_call(functools.partial(block_kernel, n), out_shape=(jax.ShapeDt...  123 us
    pallas_call x1, Pallas kernels, scan_and_smooth(): pl.pallas_call(functools.partial(scan_kernel, blocks), out_shape=(jax.Sha...  50.3 us

profile of v5, /device:TPU:0, one launch (start us, length us, event | category | flops | bytes accessed | tf_op | source)
XLA Modules:
  0.0 179.3 jit_solution(11913293078838615388)
XLA Ops:
  0.6 0.0 copy-start
  0.6 0.7 copy-done
  1.3 122.9 %shard_map.50 = (f32[4,512,512]{2,1,0:T(8,128)}, f32[4,128,512]{2,1,0:T(8,128)S(1)}, f32[4,128,512]{2,1,0:T(8,128)S(1)}, f32[528,512]{1,0:T(8,128)}, f32[4,4,128...) custom-call(f32[4,128,512]{2,1,0:T(8,128)} %e_ref.1, ...), custom_call_target="tpu_custom_call" | custom-call | flops 2415919104 | bytes 12582912 | tf_op jit(solution)/shard_map/pallas_call | solution.py:193
  124.2 0.0 copy-start.1
  124.2 1.0 copy-done.1
  125.2 2.3 %slice_bitcast_fusion.more_3_ = f32[512,512]{1,0:T(8,128)} fusion(f32[4,512,512]{2,1,0:T(8,128)} %get-tuple-element.18), kind=kLoop, calls=%fused_computation | loop fusion | bytes 2097152 | tf_op jit(solution)/shard_map/squeeze | solution.py:510
  127.5 50.3 %shard_map.51 = (f32[4,128,512]{2,1,0:T(8,128)S(1)}, f32[8,512]{1,0:T(8,128)S(1)}) custom-call(f32[528,512]{1,0:T(8,128)} %get-tuple-element.12.cov_ref, f32[512,512]{1,0:T(8,128)S(1)} %bitcast.5, f32[4,128,512]{2,1,0:T(8,128)S(1)} %get-tuple-element.14.covs_ref, f32[512,512]{1,0:T(8,128)S(1)} %get-tuple-element.15.more_0_, ...), custom_call_target="tpu_custom_call" | custom-call | flops 3221225472 | bytes 12582912 | tf_op jit(solution)/shard_map/pallas_call | solution.py:417
  177.8 0.6 add.7
  178.3 1.0 copy.6
  (3 shorter events, 0.0 us)
Async XLA Ops:
  0.6 0.7 copy-start
  124.2 1.0 copy-start.1

commit v6 on v5

--- a/solution.py
+++ b/solution.py
@@ -41,15 +41,15 @@
 
 def send_order(steps, hops):
     sends = [(k, hop) for hop in range(hops) for k in range(steps)]
-    return sorted(sends, key=lambda send: 3 * send[1] + send[0] + send[0] // 3)
+    return sorted(sends, key=lambda send: 3 * send[1] + send[0] + 4 * (send[0] // 3))
 
 
 def block_kernel(
-    n, e_ref, g_ref, l_ref, whole_ref, own_ref, covs_ref, cov_ref, offsets_ref, means_ref, *more
+    n, e_ref, g_ref, l_ref, last_ref, own_ref, covs_ref, cov_ref, offsets_ref, means_ref, *more
 ):
     steps, rows, width = e_ref.shape
     gains = more[: steps - 1]
-    (columns_ref, pieces_ref, e_send, e_recv, z_send, z_recv, c_send, c_recv, g_send,
+    (whole_ref, columns_ref, pieces_ref, e_send, e_recv, z_send, z_recv, c_send, c_recv, g_send,
      g_recv) = more[steps - 1 :]
     me = lax.axis_index("panel")
     right = lax.rem(me + 1, n)
@@ -71,7 +71,7 @@
         )
     pl.semaphore_wait(barrier, n - 1)
 
-    arrival = [steps - 2, steps - 1, *range(steps - 3, -1, -1)]
+    arrival = [*range(steps - 2, -1, -1), steps - 1]
     order = [(arrival[k], hop) for k, hop in send_order(steps, n - 1)]
     ring, landed, sent = {}, set(), []
 
@@ -117,7 +117,8 @@
 
     for k in range(steps - 2, -1, -1):
         complete(k)
-        pump(3)
+        if k > 0:
+            pump(2)
         columns_ref[k] = three_pass(whole_ref[k], covs_ref[k + 1], 1)
         swaps = []
         for d, peer in enumerate(peers):
@@ -128,10 +129,8 @@
             swap.start()
             swaps.append(swap)
         pieces_ref[k, me] = columns_ref[k, part(me)]
-        if k == steps - 2:
-            complete(steps - 1)
+        if k == 0:
             pump(len(order))
-            compose(k)
         for swap in swaps:
             swap.wait_recv()
         sent.extend(swaps)
@@ -139,7 +138,7 @@
         covs_ref[k] = three_pass(pieces, whole_ref[k], 1) + l_ref[k]
 
     kept = n // 2 + 1
-    later = list(range(steps - 3, -1, -1))
+    later = list(range(steps - 2, -1, -1))
     for j in range(kept):
         at = part(lax.rem(me + j, n))
         cov_ref[part(me), at] = covs_ref[0, :, at]
@@ -155,6 +154,8 @@
             move.start()
             moves.append(move)
         if later:
+            if hop == 0:
+                complete(steps - 1)
             compose(later.pop(0))
         for move in moves:
             move.wait_recv()
@@ -177,6 +178,7 @@
             cov_ref[p * rows : (p + 1) * rows, q * rows : (q + 1) * rows] = cov_ref[
                 q * rows : (q + 1) * rows, p * rows : (p + 1) * rows
             ].T
+    last_ref[...] = whole_ref[steps - 1]
     own_ref[steps - 1] = e_ref[steps - 1]
     for k in range(steps - 1):
         own_ref[k] = gains[k][part(me)]
@@ -193,7 +195,7 @@
     return pl.pallas_call(
         functools.partial(block_kernel, n),
         out_shape=(
-            jax.ShapeDtypeStruct((steps, width, width), f32),
+            jax.ShapeDtypeStruct((width, width), f32),
             jax.ShapeDtypeStruct((steps, rows, width), f32),
             jax.ShapeDtypeStruct((steps, rows, width), f32),
             jax.ShapeDtypeStruct((width + 16, width), f32),
@@ -204,6 +206,7 @@
         in_specs=[vmem] * 3,
         out_specs=(vmem,) * (steps + 5),
         scratch_shapes=[
+            pltpu.VMEM((steps, width, width), f32),
             pltpu.VMEM((steps - 1, width, rows), f32),
             pltpu.VMEM((steps - 1, n, rows, rows), f32),
             dma((steps, n - 1)), dma((steps, n - 1)),
@@ -504,10 +507,10 @@
     steps, rows = transitions.shape[:2]
     start = lax.axis_index("panel") * rows
     if rows % 128 == 0 and steps > 1 and lax.axis_size("tm") > 2:
-        whole, own, covs, whole_cov, _, means, *composed = block_element(
+        last, own, covs, whole_cov, _, means, *composed = block_element(
             transitions, offsets, noise_cov
         )
-        gains = [*composed, whole[steps - 1]]
+        gains = [*composed, last]
         mean, out = scan_and_smooth(whole_cov, own.reshape(steps * rows, -1), covs, gains)
         rows_mean = lax.dynamic_slice_in_dim(means[:, 0], start, rows, 1)
         return mean[0].reshape(steps, rows) + rows_mean, out

time: 180 us -> 171 us (0.950)
  Pallas kernels: 173 us -> 166 us
  local copies, waits for them, and re-layouts: 4.92 us -> 2.63 us
    pallas_call x1, Pallas kernels: 123 us -> 116 us  [block_element(): pl.pallas_call(functools.partial(block_kernel, n), out_shape=(jax.ShapeDt...]
    squeeze x1 -> x0, local copies, waits for them, and re-layouts: 2.3 us -> none  [per_device(): gains = [*composed, whole[steps - 1]]]
where the time goes in v6:
time: 171 us; the launch traced here: 170 us
  Pallas kernels  166 us (97%)
  local copies, waits for them, and re-layouts  2.63 us (2%)
    pallas_call x1, Pallas kernels, block_element(): pl.pallas_call(functools.partial(block_kernel, n), out_shape=(jax.ShapeDt...  116 us
    pallas_call x1, Pallas kernels, scan_and_smooth(): pl.pallas_call(functools.partial(scan_kernel, blocks), out_shape=(jax.Sha...  50.2 us

profile of v6, /device:TPU:0, one launch (start us, length us, event | category | flops | bytes accessed | tf_op | source)
XLA Modules:
  0.0 169.9 jit_solution(12434383936755660270)
XLA Ops:
  0.6 0.0 copy-start
  0.6 0.7 copy-done
  1.3 115.8 %shard_map.50 = (f32[512,512]{1,0:T(8,128)S(1)}, f32[4,128,512]{2,1,0:T(8,128)S(1)}, f32[4,128,512]{2,1,0:T(8,128)S(1)}, f32[528,512]{1,0:T(8,128)}, f32[4,4,128...) custom-call(f32[4,128,512]{2,1,0:T(8,128)} %e_ref.1, ...), custom_call_target="tpu_custom_call" | custom-call | flops 2415919104 | bytes 12582912 | tf_op jit(solution)/shard_map/pallas_call | solution.py:195
  117.1 0.0 copy-start.1
  117.1 1.0 copy-done.1
  118.1 50.2 %shard_map.51 = (f32[4,128,512]{2,1,0:T(8,128)S(1)}, f32[8,512]{1,0:T(8,128)S(1)}) custom-call(f32[528,512]{1,0:T(8,128)} %get-tuple-element.12.cov_ref, f32[512,512]{1,0:T(8,128)S(1)} %bitcast.3, f32[4,128,512]{2,1,0:T(8,128)S(1)} %get-tuple-element.14.covs_ref, f32[512,512]{1,0:T(8,128)S(1)} %get-tuple-element.15.more_0_, ...), custom_call_target="tpu_custom_call" | custom-call | flops 3221225472 | bytes 12582912 | tf_op jit(solution)/shard_map/pallas_call | solution.py:420
  168.4 0.6 add.7
  168.9 1.0 copy.6
  (3 shorter events, 0.0 us)
Async XLA Ops:
  0.6 0.7 copy-start
  117.1 1.0 copy-start.1

commit v7 on v6

--- a/solution.py
+++ b/solution.py
@@ -138,30 +138,19 @@
         covs_ref[k] = three_pass(pieces, whole_ref[k], 1) + l_ref[k]
 
     kept = n // 2 + 1
-    later = list(range(steps - 2, -1, -1))
-    for j in range(kept):
-        at = part(lax.rem(me + j, n))
-        cov_ref[part(me), at] = covs_ref[0, :, at]
-    for hop in range(n - 1):
-        owner = lax.rem(me - hop + n, n)
-        moves = []
-        for j in range(kept):
-            at = part(lax.rem(owner + j, n))
-            source = covs_ref.at[0, :, at] if hop == 0 else cov_ref.at[part(owner), at]
+    blocks = [part(lax.rem(me + j, n)) for j in range(kept)]
+    moves = []
+    for d, peer in enumerate(peers):
+        for j, at in enumerate(blocks):
             move = copy(
-                source, cov_ref.at[part(owner), at], c_send.at[hop, j], c_recv.at[hop, j], right
+                covs_ref.at[0, :, at], cov_ref.at[part(me), at],
+                c_send.at[d, j], c_recv.at[d, j], peer,
             )
             move.start()
             moves.append(move)
-        if later:
-            if hop == 0:
-                complete(steps - 1)
-            compose(later.pop(0))
-        for move in moves:
-            move.wait_recv()
-        sent.extend(moves)
-    for k in later:
-        compose(k)
+    sent.extend(moves)
+    for at in blocks:
+        cov_ref[part(me), at] = covs_ref[0, :, at]
     for small in smalls:
         small.wait_recv()
     for k in range(steps - 1, -1, -1):
@@ -172,6 +161,11 @@
         means_ref[k] = row
     cov_ref[width : width + 8] = means_ref[0]
     cov_ref[width + 8 :] = jnp.zeros((8, width), jnp.float32)
+    complete(steps - 1)
+    for k in range(steps - 2, -1, -1):
+        compose(k)
+    for move in moves:
+        move.wait_recv()
     for p in range(n):
         for j in range(kept, n):
             q = (p + j) % n

time: 171 us -> 170 us (level)
  Pallas kernels: 166 us -> 164 us
    pallas_call x1, Pallas kernels: 116 us -> 114 us  [block_element(): pl.pallas_call(functools.partial(block_kernel, n), out_shape=(jax.ShapeDt...]
where the time goes in v7:
time: 170 us; the launch traced here: 168 us
  Pallas kernels  164 us (96%)
  local copies, waits for them, and re-layouts  2.63 us (2%)
    pallas_call x1, Pallas kernels, block_element(): pl.pallas_call(functools.partial(block_kernel, n), out_shape=(jax.ShapeDt...  114 us
    pallas_call x1, Pallas kernels, scan_and_smooth(): pl.pallas_call(functools.partial(scan_kernel, blocks), out_shape=(jax.Sha...  50.2 us

profile of v7, /device:TPU:0, one launch (start us, length us, event | category | flops | bytes accessed | tf_op | source)
XLA Modules:
  0.0 168.0 jit_solution(4930385709380586994)
XLA Ops:
  0.6 0.0 copy-start
  0.6 0.7 copy-done
  1.3 113.9 %shard_map.50 = (f32[512,512]{1,0:T(8,128)S(1)}, f32[4,128,512]{2,1,0:T(8,128)S(1)}, f32[4,128,512]{2,1,0:T(8,128)S(1)}, f32[528,512]{1,0:T(8,128)}, f32[4,4,128...) custom-call(f32[4,128,512]{2,1,0:T(8,128)} %e_ref.1, ...), custom_call_target="tpu_custom_call" | custom-call | flops 2415919104 | bytes 12582912 | tf_op jit(solution)/shard_map/pallas_call | solution.py:189
  115.2 0.0 copy-start.1
  115.2 1.0 copy-done.1
  116.2 50.2 %shard_map.51 = (f32[4,128,512]{2,1,0:T(8,128)S(1)}, f32[8,512]{1,0:T(8,128)S(1)}) custom-call(f32[528,512]{1,0:T(8,128)} %get-tuple-element.12.cov_ref, f32[512,512]{1,0:T(8,128)S(1)} %bitcast.3, f32[4,128,512]{2,1,0:T(8,128)S(1)} %get-tuple-element.14.covs_ref, f32[512,512]{1,0:T(8,128)S(1)} %get-tuple-element.15.more_0_, ...), custom_call_target="tpu_custom_call" | custom-call | flops 3221225472 | bytes 12582912 | tf_op jit(solution)/shard_map/pallas_call | solution.py:414
  166.5 0.6 add.7
  167.1 1.0 copy.6
  (3 shorter events, 0.0 us)
Async XLA Ops:
  0.6 0.7 copy-start
  115.2 1.0 copy-start.1
